TPU v7x, 256 devices: a whole 4x4x8 slice. The times are simulated.
256 devices in a mesh: wide: 64 (over y, x_lo, z), narrow: 4 (over x_hi, core).
Axes of the slice: x: 4 (x_hi: 2, x_lo: 2; x = x_hi * 2 + x_lo), y: 4, z: 8, core: 2. Of those that a mesh axis runs over, the one named last changes fastest.
Arguments:
- displacement: float32 [3, 8, 512, 512], P(None, None, 'wide', 'narrow'), may hold values from -6 to 6
- lift_weight: float32 [3, 64], replicated, may hold values from -5 to 5
- conv1_weight: bfloat16 [3, 3, 3, 64, 64], replicated, may hold values from -0.21875 to 0.21875
- first_reduce_weight: bfloat16 [2, 2, 2, 64, 128], replicated, may hold values from -0.375 to 0.375
- conv2_weight: bfloat16 [3, 3, 3, 128, 128], replicated, may hold values from -0.15625 to 0.15625
- second_reduce_weight: bfloat16 [2, 2, 2, 128, 256], replicated, may hold values from -0.25 to 0.25
- conv3_weight: bfloat16 [3, 3, 3, 256, 256], replicated, may hold values from -0.109375 to 0.109375
Outputs:
- finest_skip_features: bfloat16 [64, 8, 512, 512], P(None, None, 'wide', 'narrow')
- middle_skip_features: bfloat16 [128, 4, 256, 256], P(None, None, 'wide', 'narrow')
- coarse_features: bfloat16 [256, 2, 128, 128], P('wide', None, None, 'narrow')
All inputs are finite; a program needn't handle non-finite values.
Results may differ from a plain program's by a relative error of at most 0.013.
Values may be sent and summed in bfloat16 or wider, within the bound.
No kernel may reach another device: no remote copies, remote signals or barrier semaphores. Data moves between devices by JAX's collectives and lax.ppermute only.
A program may use at most 128 MiB of HBM per device.

v0:
```python
import jax
import jax.numpy as jnp
from jax import lax
from jax.experimental import pallas as pl
from jax.experimental.pallas import tpu as pltpu
from jax.sharding import PartitionSpec as P

F32 = jnp.float32
BF = jnp.bfloat16
VMEM = pltpu.VMEM
LIMIT = 58 * 1024 * 1024


def leaky(v):
    return jnp.maximum(v, 0.01 * v)


def rounded(v):
    return v.astype(BF).astype(F32)


def mm(a, b):
    return jnp.dot(a, b, preferred_element_type=F32)


def call(kernel, outs, args, scratch=(), name=None, flops=0, nbytes=0, in_specs=None):
    whole = pl.BlockSpec(memory_space=VMEM)
    return pl.pallas_call(
        kernel,
        out_shape=outs,
        in_specs=[whole] * len(args) if in_specs is None else in_specs,
        out_specs=jax.tree.map(lambda _: whole, outs),
        scratch_shapes=list(scratch),
        compiler_params=pltpu.CompilerParams(vmem_limit_bytes=LIMIT),
        cost_estimate=pl.CostEstimate(flops=flops, bytes_accessed=nbytes, transcendentals=0),
        name=name,
    )(*args)


def weights_kernel(lift_ref, c1_ref, c2_ref, wl_ref, w1_ref, w2_ref):
    w = lift_ref[...]
    hi = rounded(w)
    low = rounded(w - hi)
    place = (
        lax.broadcasted_iota(jnp.int32, (64, 256), 1) % 64
        == lax.broadcasted_iota(jnp.int32, (64, 256), 0)
    ).astype(BF)
    hi4 = mm(hi.astype(BF), place)
    low4 = mm(low.astype(BF), place)
    terms = []
    for s in range(5):
        for m in range(3):
            src = low4 if s in (1, 3) else hi4
            terms.append(jnp.broadcast_to(src[m : m + 1, :], (8, 256)))
    terms.append(jnp.zeros((8, 256), F32))
    base = jnp.concatenate(terms, axis=0)
    row = lax.broadcasted_iota(jnp.int32, (128, 256), 0) % 8
    column = lax.broadcasted_iota(jnp.int32, (128, 256), 1) // 64
    for i in range(8):
        for j in range(4):
            keep = (row == i) & (column == j)
            wl_ref[i, j * 128 : (j + 1) * 128, :] = jnp.where(keep, base, 0.0).astype(BF)
    rows64 = lax.broadcasted_iota(jnp.int32, (64, 128), 0)
    lanes64 = lax.broadcasted_iota(jnp.int32, (64, 128), 1)
    left = (rows64 == lanes64).astype(BF)
    right = (rows64 + 64 == lanes64).astype(BF)
    zero1 = jnp.zeros((256, 128), BF)
    zero64 = jnp.zeros((64, 128), F32)
    for b in range(3):
        for a in range(3):
            k = c1_ref[a * 3 + b]
            pair = jnp.concatenate([mm(k, left), zero64], 0) + jnp.concatenate(
                [zero64, mm(k, right)], 0
            )
            pair = pair.astype(BF)
            w1_ref[a * 3 + b, :, 0:128] = pair
            w1_ref[(a + 1) * 3 + b, :, 128:256] = pair
        w1_ref[9 + b, :, 0:128] = zero1
        w1_ref[b, :, 128:256] = zero1
    zero2 = jnp.zeros((384, 128), BF)
    for b in range(3):
        for a in range(3):
            w2_ref[a * 3 + b, :, 0:128] = c2_ref[a * 3 + b]
            w2_ref[(a + 1) * 3 + b, :, 128:256] = c2_ref[a * 3 + b]
        w2_ref[9 + b, :, 0:128] = zero2
        w2_ref[b, :, 128:256] = zero2


def turn_kernel(up_ref, own_ref, down_ref, dt_ref, left_ref, right_ref):
    for plane in range(8):
        for blk, src in enumerate((up_ref, own_ref, down_ref)):
            parts = [[], [], []]
            for m in range(3):
                v = src[m * 8 + plane]
                hi = rounded(v)
                rest = v - hi
                mid = rounded(rest)
                parts[0].append(hi)
                parts[1].append(mid)
                parts[2].append(rest - mid)
            tiles = parts[0] + parts[0] + parts[1] + parts[1] + parts[2]
            tiles.append(jnp.zeros((8, 128), F32))
            turned = jnp.concatenate(tiles, axis=0).T
            g = plane * 3 + blk
            dt_ref[g, 8:136] = turned
            left_ref[g] = turned[0:8]
            right_ref[g] = turned[120:128]
    dt_ref[:, 0:8, :] = jnp.zeros((24, 8, 128), F32)
    dt_ref[:, 136:144, :] = jnp.zeros((24, 8, 128), F32)


def fine_levels(lhs_ref, wl_ref, w1_ref, wr1_ref, x4_ref, fn_ref, mid_ref, pairs, chunk):
    zero = jnp.zeros((24, pairs, 256), BF)
    x4_ref[0] = zero
    x4_ref[9] = zero

    def lift(i, carry):
        out = leaky(mm(lhs_ref[...], wl_ref[i])).astype(BF)
        for g in range(24):
            x4_ref[1 + g // 3, (g % 3) * 8 + i] = out[g * pairs : (g + 1) * pairs]
        return carry

    lax.fori_loop(0, 8, lift, 0)
    weight = w1_ref[...].reshape(3072, 256)

    def conv(pp, carry):
        for r0 in range(0, 20, chunk):
            lhs = jnp.concatenate(
                [
                    x4_ref[2 * pp + dp, 1 + b + r0 : 1 + b + r0 + chunk].reshape(
                        chunk * pairs, 256
                    )
                    for dp in range(4)
                    for b in range(3)
                ],
                axis=1,
            )
            out = leaky(mm(lhs, weight)).astype(BF)
            for q in range(2):
                fn_ref[2 * pp + q, r0 // 2 : (r0 + chunk) // 2] = out[
                    :, q * 128 : (q + 1) * 128
                ].reshape(chunk // 2, 2, pairs, 128)
        lhs = jnp.concatenate(
            [
                fn_ref[2 * pp + a, :, b].reshape(10 * pairs, 128)
                for a in range(2)
                for b in range(2)
            ],
            axis=1,
        )
        out = leaky(mm(lhs, wr1_ref[...]))
        mid_ref[pp] = out.astype(mid_ref.dtype).reshape(10, pairs, 128)
        return carry

    lax.fori_loop(0, 4, conv, 0)


def inner_kernel(dt_ref, wl_ref, w1_ref, wr1_ref, fin_ref, mid_ref, lhs_ref, x4_ref, fn_ref):
    def gather(g, carry):
        lhs_ref[pl.ds(pl.multiple_of(g * 64, 64), 64), :] = jnp.concatenate(
            [dt_ref[g, pl.ds(7 + j, 64, stride=2)] for j in range(4)], axis=1
        ).astype(BF)
        return carry

    lax.fori_loop(0, 24, gather, 0)
    fine_levels(lhs_ref, wl_ref, w1_ref, wr1_ref, x4_ref, fn_ref, mid_ref, 64, 10)
    for plane in range(8):
        fin_ref[plane] = fn_ref[plane, 3:7].reshape(8, 64, 128)


def outer_kernel(
    lrecv_ref, left_ref, right_ref, rrecv_ref, wl_ref, w1_ref, wr1_ref, main_ref, w2_hbm, wr2_hbm, w3_hbm,
    edge_ref, skip_ref, chunk_ref,
    de_ref, lhs_ref, x4_ref, fn_ref, me_ref, mf_ref, xm_ref, ms_ref, cf_ref, w2_ref, wr2_ref, w3_ref, sems,
):
    copies = [
        pltpu.make_async_copy(src, dst, sems.at[n])
        for n, (src, dst) in enumerate(((w2_hbm, w2_ref), (wr2_hbm, wr2_ref), (w3_hbm, w3_ref)))
    ]
    for copy in copies:
        copy.start()
    de_ref[:, 0:8] = lrecv_ref[...]
    de_ref[:, 8:16] = left_ref[...]
    de_ref[:, 16:24] = right_ref[...]
    de_ref[:, 24:32] = rrecv_ref[...]
    de_ref[:, 32:40] = jnp.zeros((24, 8, 128), F32)
    for g in range(24):
        lhs_ref[g * 16 : (g + 1) * 16, :] = jnp.concatenate(
            [
                jnp.concatenate(
                    [
                        de_ref[g, pl.ds(1 + j, 8, stride=2)],
                        de_ref[g, pl.ds(21 + j, 8, stride=2)],
                    ],
                    axis=0,
                )
                for j in range(4)
            ],
            axis=1,
        ).astype(BF)
    fine_levels(lhs_ref, wl_ref, w1_ref, wr1_ref, x4_ref, fn_ref, me_ref, 16, 20)
    for plane in range(8):
        edge_ref[plane] = fn_ref[plane, 3:7].reshape(8, 16, 128)

    def merge(n, carry):
        plane, row = n // 10, n % 10
        mf_ref[n, 3:67] = main_ref[plane, row].astype(F32)
        mf_ref[n, 0:4] = me_ref[plane, row, 0:4]
        mf_ref[n, 66:70] = me_ref[plane, row, 8:12]
        for c in range(3):
            xm_ref[plane, row, :, c * 128 : (c + 1) * 128] = mf_ref[n, c : c + 80].astype(BF)
        return carry

    lax.fori_loop(0, 40, merge, 0)
    copies[0].wait()
    for half in range(2):
        taps = range(1, 4) if half == 0 else range(0, 3)
        lhs = jnp.concatenate(
            [
                xm_ref[2 * half - 1 + dp, b : b + 8].reshape(640, 384)
                for dp in taps
                for b in range(3)
            ],
            axis=1,
        )
        weight = w2_ref[taps[0] * 3 : taps[0] * 3 + 9].reshape(3456, 256)
        out = rounded(leaky(mm(lhs, weight)))
        for q in range(2):
            ms_ref[2 * half + q] = out[:, q * 128 : (q + 1) * 128].reshape(8, 80, 128)
    for plane in range(4):
        for row in range(4):
            skip_ref[plane, row] = ms_ref[plane, row + 2, 2:66].astype(BF)
    copies[1].wait()
    taps = []
    for a in range(2):
        for b in range(2):
            for c in range(2):
                taps.append(
                    jnp.concatenate(
                        [
                            ms_ref[2 * plane + a, 2 * row + b, pl.ds(c, 40, stride=2)]
                            for plane in range(2)
                            for row in range(4)
                        ],
                        axis=0,
                    )
                )
    lhs = jnp.concatenate(taps, axis=1).astype(BF)
    out = rounded(leaky(mm(lhs, wr2_ref[...])))
    cf_ref[...] = out.reshape(2, 4, 40, 256)
    lhs = []
    for plane in range(2):
        lhs.append(
            jnp.concatenate(
                [
                    jnp.concatenate(
                        [cf_ref[plane, row + b, c : c + 32] for row in range(2)], axis=0
                    )
                    for b in range(3)
                    for c in range(3)
                ],
                axis=1,
            ).astype(BF)
        )
    copies[2].wait()
    same = mm(jnp.concatenate(lhs, axis=0), w3_ref[1])
    first = same[0:64] + mm(lhs[1], w3_ref[2])
    second = same[64:128] + mm(lhs[0], w3_ref[0])
    out = jnp.concatenate([first[0:32], second[0:32], first[32:64], second[32:64]], axis=0)
    out = leaky(out).T
    chunk_ref[...] = out.reshape(64, 4, 128)


def finest_kernel(fin_ref, edge_ref, out_ref, wide_ref, tile_ref):
    lane = lax.broadcasted_iota(jnp.int32, (64, 128), 1)
    for row in range(0, 8, 2):
        now = []
        for r in (row, row + 1):
            tile_ref[...] = fin_ref[0, r].astype(F32)
            tile_ref[0:1] = edge_ref[0, r, 3:4].astype(F32)
            tile_ref[63:64] = edge_ref[0, r, 8:9].astype(F32)
            now.append(tile_ref[...])
        even = jnp.where(lane < 64, now[0], pltpu.roll(now[1], 64, 1))
        odd = jnp.where(lane < 64, pltpu.roll(now[0], 64, 1), now[1])
        wide_ref[pl.ds(0, 64, stride=2), :] = even
        wide_ref[pl.ds(1, 64, stride=2), :] = odd
        turned = wide_ref[...].T
        out_ref[:, 0, row, :] = turned[0:64].astype(out_ref.dtype)
        out_ref[:, 0, row + 1, :] = turned[64:128].astype(out_ref.dtype)


def coarse_kernel(in_ref, out_ref, y_ref):
    for c in range(4):
        v = in_ref[:, c, :]
        y_ref[pl.ds(0, 64, stride=2), :] = v
        y_ref[pl.ds(1, 64, stride=2), :] = pltpu.roll(v, 64, 1)
        out_ref[c] = y_ref[...].T[0:64].reshape(2, 32, 128).astype(BF)


def shift(array, axis, step):
    peers = lax.axis_size(axis)
    return lax.ppermute(array, axis, [(i, (i + step) % peers) for i in range(peers)])


def struct(shape, dtype):
    return jax.ShapeDtypeStruct(shape, dtype)


def on_device(disp, lift_w, conv1_w, reduce1_w, conv2_w, reduce2_w, conv3_w):
    own = disp.reshape(24, 8, 128)
    up = shift(own, "wide", 1)
    wl, w1, w2 = call(
        weights_kernel,
        (struct((8, 512, 256), BF), struct((12, 256, 256), BF), struct((12, 384, 256), BF)),
        (lift_w, conv1_w.reshape(9, 192, 64), conv2_w.reshape(9, 384, 128)),
        name="arrange_weights",
        flops=10**9,
        nbytes=7 * 10**6,
    )
    down = shift(own, "wide", -1)
    dt, left, right = call(
        turn_kernel,
        (struct((24, 144, 128), F32), struct((24, 8, 128), F32), struct((24, 8, 128), F32)),
        (up, own, down),
        name="columns_to_rows",
        flops=10**7,
        nbytes=2 * 10**6,
    )
    rrecv = shift(left, "narrow", -1)
    lrecv = shift(right, "narrow", 1)
    wr1 = reduce1_w.reshape(512, 128)
    fin, mid = call(
        inner_kernel,
        (struct((8, 8, 64, 128), BF), struct((4, 10, 64, 128), BF)),
        (dt, wl, w1, wr1),
        scratch=(
            VMEM((1536, 512), BF),
            VMEM((10, 24, 64, 256), BF),
            VMEM((8, 10, 2, 64, 128), BF),
        ),
        name="fine_inner",
        flops=8 * 10**9,
        nbytes=8 * 10**6,
    )
    hbm = pl.BlockSpec(memory_space=pl.ANY)
    whole = pl.BlockSpec(memory_space=VMEM)
    edge, skip, chunk = call(
        outer_kernel,
        (struct((8, 8, 16, 128), BF), struct((4, 4, 64, 128), BF), struct((64, 4, 128), F32)),
        (
            lrecv, left, right, rrecv, wl, w1, wr1, mid, w2,
            reduce2_w.reshape(1024, 256), conv3_w.reshape(3, 2304, 256),
        ),
        in_specs=[whole] * 8 + [hbm] * 3,
        scratch=(
            VMEM((24, 40, 128), F32),
            VMEM((384, 512), BF),
            VMEM((10, 24, 16, 256), BF),
            VMEM((8, 10, 2, 16, 128), BF),
            VMEM((4, 10, 16, 128), F32),
            VMEM((40, 88, 128), F32),
            VMEM((4, 10, 80, 384), BF),
            VMEM((4, 8, 80, 128), F32),
            VMEM((2, 4, 40, 256), F32),
            VMEM((12, 384, 256), BF),
            VMEM((1024, 256), BF),
            VMEM((3, 2304, 256), BF),
            pltpu.SemaphoreType.DMA((3,)),
        ),
        name="middle_and_coarse",
        flops=6 * 10**9,
        nbytes=12 * 10**6,
    )
    received = lax.all_to_all(chunk, "wide", 0, 0, tiled=True)
    finest = pl.pallas_call(
        finest_kernel,
        grid=(8,),
        out_shape=struct((64, 8, 8, 128), BF),
        in_specs=[
            pl.BlockSpec((1, 8, 64, 128), lambda p: (p, 0, 0, 0)),
            pl.BlockSpec((1, 8, 16, 128), lambda p: (p, 0, 0, 0)),
        ],
        out_specs=pl.BlockSpec((64, 1, 8, 128), lambda p: (0, p, 0, 0)),
        scratch_shapes=[VMEM((128, 128), F32), VMEM((64, 128), F32)],
        compiler_params=pltpu.CompilerParams(vmem_limit_bytes=LIMIT),
        cost_estimate=pl.CostEstimate(flops=10**8, bytes_accessed=3 * 10**6, transcendentals=0),
        name="finest_layout",
    )(fin, edge)
    coarse = call(
        coarse_kernel,
        struct((4, 2, 32, 128), BF),
        (received,),
        scratch=(VMEM((128, 128), F32),),
        name="coarse_layout",
        flops=10**6,
        nbytes=2 * 10**5,
    )
    return finest, skip.transpose(3, 0, 1, 2), coarse.transpose(0, 1, 3, 2)


def solution(mesh):
    return jax.shard_map(
        on_device,
        mesh=mesh,
        in_specs=(P(None, None, "wide", "narrow"), P(), P(), P(), P(), P(), P()),
        out_specs=(
            P(None, None, "wide", "narrow"),
            P(None, None, "wide", "narrow"),
            P("wide", None, None, "narrow"),
        ),
        check_vma=False,
    )
```

profile of v0, /device:TPU:4, one launch (start us, length us, event | category | flops | bytes accessed | tf_op | source)
XLA Modules:
  0.0 77.5 jit_solution(1513000167963772694)
XLA Ops:
  0.6 2.0 %collective-permute-start = (f32[24,8,128]{2,1,0:T(8,128)}, f32[24,8,128]{2,1,0:T(8,128)S(1)}, u32[]{:S(2)}, u32[]{:S(2)}) collective-permute-start(f32[24,8,128]{2,1,0:T(8,128)} %bitcast.8), channel_id=1, source_target_pairs={{0,4},{4,8},{8,12},{12,16},{16,20},{20,24},{24,28},{28,32},{32,36}... | collective-permute-start | bytes 294920 | tf_op jit(solution)/shard_map/ppermute | solution.py:302
  2.6 7.1 %collective-permute-start.1 = (f32[24,8,128]{2,1,0:T(8,128)}, f32[24,8,128]{2,1,0:T(8,128)S(1)}, u32[]{:S(2)}, u32[]{:S(2)}) collective-permute-start(f32[24,8,128]{2,1,0:T(8,128)} %bitcast.9), channel_id=1, source_target_pairs={{0,252},{4,0},{8,4},{12,8},{16,12},{20,16},{24,20},{28,24},{32,28}... | collective-permute-start | bytes 294920 | tf_op jit(solution)/shard_map/ppermute | solution.py:302
  9.7 4.5 %arrange_weights.1 = (bf16[8,512,256]{2,1,0:T(8,128)(2,1)}, bf16[12,256,256]{2,1,0:T(8,128)(2,1)}, bf16[12,384,256]{2,1,0:T(8,128)(2,1)}) custom-call(f32[3,64]{1,0:T(4,128)} %lift_ref.1, bf16[9,192,64]{2,1,0:T(8,128)(2,1)} %bitcast.15, bf16[9,384,128]{2,1,0:T(8,128)(2,1)} %bitcast.13), custom_call_target="tpu_custom_call" | custom-call | flops 1000000000 | bytes 7000000 | tf_op jit(solution)/shard_map/arrange_weights/pallas_call | solution.py:28
  14.2 0.0 collective-permute-done.up_ref
  14.2 0.0 copy-start.1
  14.2 0.0 collective-permute-done.1.down_ref
  14.2 0.6 copy-done.1
  14.9 0.0 copy-start.2
  14.9 0.6 copy-done.2
  15.5 2.7 %columns_to_rows.1 = (f32[24,144,128]{2,1,0:T(8,128)}, f32[24,8,128]{2,1,0:T(8,128)}, f32[24,8,128]{2,1,0:T(8,128)}) custom-call(f32[24,8,128]{2,1,0:T(8,128)} %copy-done.1, f32[24,8,128]{2,1,0:T(8,128)} %bitcast.10, f32[24,8,128]{2,1,0:T(8,128)} %copy-done.2), custom_call_target="tpu_custom_call" | custom-call | flops 10000000 | bytes 2000000 | tf_op jit(solution)/shard_map/columns_to_rows/pallas_call | solution.py:28
  18.2 0.0 collective-permute-start.2
  18.2 3.2 %collective-permute-start.3 = (f32[24,8,128]{2,1,0:T(8,128)}, f32[24,8,128]{2,1,0:T(8,128)S(1)}, u32[]{:S(2)}, u32[]{:S(2)}) collective-permute-start(f32[24,8,128]{2,1,0:T(8,128)} %get-tuple-element.19.left_ref), channel_id=1, source_target_pairs={{0,3},{1,0},{2,1},{3,2},{4,7},{5,4},{6,5},{7,6},{8,11},{9,8},{10,9... | collective-permute-start | bytes 294920 | tf_op jit(solution)/shard_map/ppermute | solution.py:302
  21.5 19.8 %fine_inner.1 = (bf16[8,8,64,128]{3,2,1,0:T(8,128)(2,1)}, bf16[4,10,64,128]{3,2,1,0:T(8,128)(2,1)}) custom-call(f32[24,144,128]{2,1,0:T(8,128)} %get-tuple-element.14.dt_ref, bf16[8,512,256]{2,1,0:T(8,128)(2,1)} %get-tuple-element.15.wl_ref, bf16[12,256,256]{2,1,0:T(8,128)(2,1)} %get-tuple-element.16.w1_ref, bf16[512,128]{1,0:T(8,128)(2,1)} %bitcast.16), custom_call_target="tpu_custom_call" | custom-call | flops 8000000000 | bytes 8000000 | tf_op jit(solution)/shard_map/fine_inner/pallas_call | solution.py:28
  41.3 0.0 collective-permute-done.2.lrecv_ref
  41.3 0.0 collective-permute-done.3.rrecv_ref
  41.3 0.0 copy-start.4
  41.3 0.6 copy-done.3
  41.9 0.0 copy-done.4
  42.0 14.9 %middle_and_coarse.1 = (bf16[8,8,16,128]{3,2,1,0:T(8,128)(2,1)}, bf16[4,4,64,128]{3,2,1,0:T(8,128)(2,1)}, f32[64,4,128]{2,1,0:T(4,128)}) custom-call(f32[24,8,128]{2,1,0:T(8,128)} %copy-done.3, f32[24,8,128]{2,1,0:T(8,128)} %get-tuple-element.19.left_ref, f32[24,8,128]{2,1,0:T(8,128)} %get-tuple-element.18.right_ref, f32[24,8,128]{2,1,0:T(8,128)} %copy-done.4, ...), custom_call_target="tpu_custom_call" | custom-call | flops 6000000000 | bytes 12000000 | tf_op jit(solution)/shard_map/middle_and_coarse/pallas_call | solution.py:28
  56.9 7.0 %all-to-all-start = ((f32[64,4,128]{2,1,0:T(4,128)}), f32[64,4,128]{2,1,0:T(4,128)S(1)}, u32[]{:S(2)}, u32[]{:S(2)}) async-start(f32[64,4,128]{2,1,0:T(4,128)} %get-tuple-element.24), calls=%async_computation | async-start | bytes 262144 | tf_op jit(solution)/shard_map/all_to_all | solution.py:374
  63.8 7.2 %finest_layout.1 = bf16[64,8,8,128]{3,2,1,0:T(8,128)(2,1)} custom-call(bf16[8,8,64,128]{3,2,1,0:T(8,128)(2,1)} %get-tuple-element.17.fin_ref, bf16[8,8,16,128]{3,2,1,0:T(8,128)(2,1)} %get-tuple-element.22.edge_ref), custom_call_target="tpu_custom_call" | custom-call | flops 100000000 | bytes 3000000 | tf_op jit(solution)/shard_map/finest_layout/pallas_call | solution.py:375
  71.1 4.0 %all-to-all-done.in_ref = f32[64,4,128]{2,1,0:T(4,128)S(1)} async-done(((f32[64,4,128]{2,1,0:T(4,128)}), f32[64,4,128]{2,1,0:T(4,128)S(1)}, u32[]{:S(2)}, u32[]{:S(2)}) %all-to-all-start) | async-done | bytes 131104 | tf_op jit(solution)/shard_map/all_to_all | solution.py:374
  75.0 0.6 copy-done
  75.7 1.8 %coarse_layout.1 = bf16[4,2,32,128]{3,2,1,0:T(8,128)(2,1)} custom-call(f32[64,4,128]{2,1,0:T(4,128)} %copy-done), custom_call_target="tpu_custom_call" | custom-call | flops 1000000 | bytes 200000 | tf_op jit(solution)/shard_map/coarse_layout/pallas_call | solution.py:28
  (2 shorter events, 0.0 us)
Async XLA Ops:
  0.6 13.6 %collective-permute-start = (f32[24,8,128]{2,1,0:T(8,128)}, f32[24,8,128]{2,1,0:T(8,128)S(1)}, u32[]{:S(2)}, u32[]{:S(2)}) collective-permute-start(f32[24,8,128]{2,1,0:T(8,128)} %bitcast.8), channel_id=1, source_target_pairs={{0,4},{4,8},{8,12},{12,16},{16,20},{20,24},{24,28},{28,32},{32,36}... | collective-permute-start | bytes 294920 | tf_op jit(solution)/shard_map/ppermute | solution.py:302
  2.6 11.6 %collective-permute-start.1 = (f32[24,8,128]{2,1,0:T(8,128)}, f32[24,8,128]{2,1,0:T(8,128)S(1)}, u32[]{:S(2)}, u32[]{:S(2)}) collective-permute-start(f32[24,8,128]{2,1,0:T(8,128)} %bitcast.9), channel_id=1, source_target_pairs={{0,252},{4,0},{8,4},{12,8},{16,12},{20,16},{24,20},{28,24},{32,28}... | collective-permute-start | bytes 294920 | tf_op jit(solution)/shard_map/ppermute | solution.py:302
  14.2 0.6 copy-start.1
  14.9 0.6 copy-start.2
  18.2 23.1 %collective-permute-start.2 = (f32[24,8,128]{2,1,0:T(8,128)}, f32[24,8,128]{2,1,0:T(8,128)S(1)}, u32[]{:S(2)}, u32[]{:S(2)}) collective-permute-start(f32[24,8,128]{2,1,0:T(8,128)} %get-tuple-element.18.right_ref), channel_id=1, source_target_pairs={{0,1},{1,2},{2,3},{3,0},{4,5},{5,6},{6,7},{7,4},{8,9},{9,10},{10,1... | collective-permute-start | bytes 294920 | tf_op jit(solution)/shard_map/ppermute | solution.py:302
  18.2 23.1 %collective-permute-start.3 = (f32[24,8,128]{2,1,0:T(8,128)}, f32[24,8,128]{2,1,0:T(8,128)S(1)}, u32[]{:S(2)}, u32[]{:S(2)}) collective-permute-start(f32[24,8,128]{2,1,0:T(8,128)} %get-tuple-element.19.left_ref), channel_id=1, source_target_pairs={{0,3},{1,0},{2,1},{3,2},{4,7},{5,4},{6,5},{7,6},{8,11},{9,8},{10,9... | collective-permute-start | bytes 294920 | tf_op jit(solution)/shard_map/ppermute | solution.py:302
  41.3 0.6 copy-start.3
  41.3 0.7 copy-start.4
  56.9 18.2 %all-to-all-start = ((f32[64,4,128]{2,1,0:T(4,128)}), f32[64,4,128]{2,1,0:T(4,128)S(1)}, u32[]{:S(2)}, u32[]{:S(2)}) async-start(f32[64,4,128]{2,1,0:T(4,128)} %get-tuple-element.24), calls=%async_computation | async-start | bytes 262144 | tf_op jit(solution)/shard_map/all_to_all | solution.py:374
  75.0 0.7 copy-start
where the time goes:
time: 77.9 us; the launch traced here: 77.5 us
  Pallas kernels  51 us (65%)
  starting transfers between devices  19.3 us (25%)
  waiting for transfers between devices  3.97 us (5%)
  local copies, waits for them, and re-layouts  2.58 us (3%)
    pallas_call x5, Pallas kernels, call(): pl.pallas_call(kernel, out_shape=outs, in_specs=[whole] * len(args) if in...  43.7 us
    ppermute x4, starting transfers between devices, shift(): lax.ppermute(array, axis, [(i, (i + step) % peers) for i in range(peers)])  12.4 us
    pallas_call x1, Pallas kernels, on_device(): pl.pallas_call(finest_kernel, grid=(8,), out_shape=struct((64, 8, 8, 128)...  7.25 us
    all_to_all x1, starting transfers between devices, on_device(): received = lax.all_to_all(chunk, 'wide', 0, 0, tiled=True)  6.95 us
    all_to_all x1, waiting for transfers between devices, on_device(): received = lax.all_to_all(chunk, 'wide', 0, 0, tiled=True)  3.96 us
    unnamed x10, local copies, waits for them, and re-layouts  2.58 us
  transfers between devices with their start and end apart: 5, of which 1 were waited for; matrix products, arithmetic and copies ran while one was open for 0% of the time, Pallas kernels for 41%

commit v1 on v0

v1 whole, which is shorter than its diff:
```python
import jax
import jax.numpy as jnp
from jax import lax
from jax.experimental import pallas as pl
from jax.experimental.pallas import tpu as pltpu
from jax.sharding import PartitionSpec as P

F32 = jnp.float32
BF = jnp.bfloat16
VMEM = pltpu.VMEM
MIB = 1024 * 1024


def leaky(v):
    return jnp.maximum(v, 0.01 * v)


def rounded(v):
    return v.astype(BF).astype(F32)


def mm(a, b):
    return jnp.dot(a, b, preferred_element_type=F32)


def call(kernel, outs, args, limit, scratch=(), name=None, flops=0, nbytes=0):
    whole = pl.BlockSpec(memory_space=VMEM)
    return pl.pallas_call(
        kernel,
        out_shape=outs,
        in_specs=[whole] * len(args),
        out_specs=jax.tree.map(lambda _: whole, outs),
        scratch_shapes=list(scratch),
        compiler_params=pltpu.CompilerParams(vmem_limit_bytes=limit * MIB),
        cost_estimate=pl.CostEstimate(flops=flops, bytes_accessed=nbytes, transcendentals=0),
        name=name,
    )(*args)


def fine_weights_kernel(lift_ref, c1_ref, wl_ref, w1_ref):
    w = lift_ref[...]
    hi = rounded(w)
    low = rounded(w - hi)
    place = (
        lax.broadcasted_iota(jnp.int32, (64, 256), 1) % 64
        == lax.broadcasted_iota(jnp.int32, (64, 256), 0)
    ).astype(BF)
    hi4 = mm(hi.astype(BF), place)
    low4 = mm(low.astype(BF), place)
    terms = []
    for s in range(5):
        for m in range(3):
            src = low4 if s in (1, 3) else hi4
            terms.append(jnp.broadcast_to(src[m : m + 1, :], (8, 256)))
    terms.append(jnp.zeros((8, 256), F32))
    base = jnp.concatenate(terms, axis=0)
    row = lax.broadcasted_iota(jnp.int32, (128, 256), 0) % 8
    lane = lax.broadcasted_iota(jnp.int32, (128, 256), 1)
    for t in range(4):
        for j in range(2):
            keep = (row == 2 * t + lane // 128) & (lane // 64 % 2 == j)
            wl_ref[t, j * 128 : (j + 1) * 128, :] = jnp.where(keep, base, 0.0).astype(BF)
    rows64 = lax.broadcasted_iota(jnp.int32, (64, 128), 0)
    lanes64 = lax.broadcasted_iota(jnp.int32, (64, 128), 1)
    left = (rows64 == lanes64).astype(BF)
    right = (rows64 + 64 == lanes64).astype(BF)
    zero1 = jnp.zeros((256, 128), BF)
    zero64 = jnp.zeros((64, 128), F32)
    for b in range(3):
        for a in range(3):
            k = c1_ref[a * 3 + b]
            pair = jnp.concatenate([mm(k, left), zero64], 0) + jnp.concatenate(
                [zero64, mm(k, right)], 0
            )
            pair = pair.astype(BF)
            w1_ref[a * 3 + b, :, 0:128] = pair
            w1_ref[(a + 1) * 3 + b, :, 128:256] = pair
        w1_ref[9 + b, :, 0:128] = zero1
        w1_ref[b, :, 128:256] = zero1


def middle_weights_kernel(c2_ref, w2_ref):
    zero2 = jnp.zeros((384, 128), BF)
    for b in range(3):
        for a in range(3):
            w2_ref[a * 3 + b, :, 0:128] = c2_ref[a * 3 + b]
            w2_ref[(a + 1) * 3 + b, :, 128:256] = c2_ref[a * 3 + b]
        w2_ref[9 + b, :, 0:128] = zero2
        w2_ref[b, :, 128:256] = zero2


def turn_kernel(up_ref, own_ref, down_ref, dt_ref, left_ref, right_ref):
    for plane in range(8):
        for blk, src in enumerate((up_ref, own_ref, down_ref)):
            parts = [[], [], []]
            for m in range(3):
                v = src[m * 8 + plane]
                hi = rounded(v)
                rest = v - hi
                mid = rounded(rest)
                parts[0].append(hi)
                parts[1].append(mid)
                parts[2].append(rest - mid)
            tiles = parts[0] + parts[0] + parts[1] + parts[1] + parts[2]
            tiles.append(jnp.zeros((8, 128), F32))
            turned = jnp.concatenate(tiles, axis=0).T
            g = plane * 3 + blk
            dt_ref[g, 8:136] = turned
            left_ref[g] = turned[0:8]
            right_ref[g] = turned[120:128]
    dt_ref[:, 0:8, :] = jnp.zeros((24, 8, 128), F32)
    dt_ref[:, 136:144, :] = jnp.zeros((24, 8, 128), F32)


def fine_levels(lhs_ref, wl_ref, w1_ref, wr1_ref, x4_ref, fn_ref, mid_ref, pairs, chunk):
    for t in range(4):
        for half in range(2):
            out = leaky(mm(lhs_ref[half], wl_ref[t])).astype(BF).astype(x4_ref.dtype)
            out = out.reshape(24, pairs, 256)
            lanes = slice(half * 128, (half + 1) * 128)
            for g in range(24):
                for r in range(2):
                    x4_ref[g // 3, (g % 3) * 8 + 2 * t + r, :, lanes] = out[
                        g, :, r * 128 : (r + 1) * 128
                    ]
    for pp in range(4):
        taps = [dp for dp in range(4) if 0 <= 2 * pp - 1 + dp < 8]
        weight = w1_ref[taps[0] * 3 : taps[-1] * 3 + 3].reshape(len(taps) * 768, 256)
        for r0 in range(0, 20, chunk):
            lhs = jnp.concatenate(
                [
                    x4_ref[2 * pp - 1 + dp, 1 + b + r0 : 1 + b + r0 + chunk].reshape(
                        chunk * pairs, 256
                    )
                    for dp in taps
                    for b in range(3)
                ],
                axis=1,
            ).astype(BF)
            out = leaky(mm(lhs, weight)).astype(BF).astype(fn_ref.dtype)
            for q in range(2):
                fn_ref[2 * pp + q, r0 // 2 : (r0 + chunk) // 2] = out[
                    :, q * 128 : (q + 1) * 128
                ].reshape(chunk // 2, 2, pairs, 128)
        lhs = jnp.concatenate(
            [
                fn_ref[2 * pp + a, :, b].reshape(10 * pairs, 128)
                for a in range(2)
                for b in range(2)
            ],
            axis=1,
        ).astype(BF)
        out = leaky(mm(lhs, wr1_ref[...])).astype(BF)
        mid_ref[pp] = out.astype(mid_ref.dtype).reshape(10, pairs, 128)


def inner_kernel(dt_ref, wl_ref, w1_ref, wr1_ref, fin_ref, mid_ref, lhs_ref, x4_ref, fn_ref):
    for g in range(24):
        for half in range(2):
            lhs_ref[half, g * 64 : (g + 1) * 64, :] = jnp.concatenate(
                [dt_ref[g, pl.ds(7 + 2 * half + j, 64, stride=2)] for j in range(2)], axis=1
            ).astype(BF)
    fine_levels(lhs_ref, wl_ref, w1_ref, wr1_ref, x4_ref, fn_ref, mid_ref, 64, 10)
    for plane in range(8):
        fin_ref[plane] = fn_ref[plane, 3:7].reshape(8, 64, 128)


def outer_kernel(
    lrecv_ref, left_ref, right_ref, rrecv_ref, wl_ref, w1_ref, wr1_ref, main_ref, w2_ref, wr2_ref, w3_ref,
    edge_ref, skip_ref, chunk_ref,
    de_ref, dw_ref, lhs_ref, x4_ref, fn_ref, me_ref, mf_ref, xm_ref, ms_ref, cf_ref,
):
    de_ref[:, 0:8] = lrecv_ref[...]
    de_ref[:, 8:16] = left_ref[...]
    de_ref[:, 16:24] = right_ref[...]
    de_ref[:, 24:32] = rrecv_ref[...]
    for half in range(2):
        dw_ref[half, :, 0:8] = de_ref[:, 1 + 2 * half : 9 + 2 * half]
        dw_ref[half, :, 8:16] = de_ref[:, 21 + 2 * half : 29 + 2 * half]
    for half in range(2):
        for g in range(0, 24, 2):
            lhs_ref[half, g * 8 : (g + 2) * 8, :] = jnp.concatenate(
                [
                    jnp.concatenate(
                        [dw_ref[half, g + k, pl.ds(j, 8, stride=2)] for k in range(2)], axis=0
                    )
                    for j in range(2)
                ],
                axis=1,
            ).astype(BF)
    fine_levels(lhs_ref, wl_ref, w1_ref, wr1_ref, x4_ref, fn_ref, me_ref, 8, 20)
    for plane in range(8):
        edge_ref[plane] = fn_ref[plane, 3:7].reshape(8, 8, 128)

    def merge(n, carry):
        plane, row = n // 10, n % 10
        mf_ref[n, 3:67] = main_ref[plane, row].astype(F32)
        mf_ref[n, 0:4] = me_ref[plane, row, 0:4]
        mf_ref[n, 66:70] = me_ref[plane, row, 4:8]
        for c in range(3):
            xm_ref[plane, row, :, c * 128 : (c + 1) * 128] = mf_ref[n, c : c + 80].astype(BF)
        return carry

    lax.fori_loop(0, 40, merge, 0)
    for half in range(2):
        taps = range(1, 4) if half == 0 else range(0, 3)
        lhs = jnp.concatenate(
            [
                xm_ref[2 * half - 1 + dp, b : b + 8].reshape(640, 384)
                for dp in taps
                for b in range(3)
            ],
            axis=1,
        )
        weight = w2_ref[taps[0] * 3 : taps[0] * 3 + 9].reshape(3456, 256)
        out = rounded(leaky(mm(lhs, weight)))
        for q in range(2):
            ms_ref[2 * half + q] = out[:, q * 128 : (q + 1) * 128].reshape(8, 80, 128)
    for plane in range(4):
        for row in range(4):
            skip_ref[plane, row] = ms_ref[plane, row + 2, 2:66].astype(BF)
    taps = []
    for a in range(2):
        for b in range(2):
            for c in range(2):
                taps.append(
                    jnp.concatenate(
                        [
                            ms_ref[2 * plane + a, 2 * row + b, pl.ds(c, 40, stride=2)]
                            for plane in range(2)
                            for row in range(4)
                        ],
                        axis=0,
                    )
                )
    lhs = jnp.concatenate(taps, axis=1).astype(BF)
    out = rounded(leaky(mm(lhs, wr2_ref[...])))
    cf_ref[...] = out.reshape(2, 4, 40, 256)
    lhs = []
    for plane in range(2):
        lhs.append(
            jnp.concatenate(
                [
                    jnp.concatenate(
                        [cf_ref[plane, row + b, c : c + 32] for row in range(2)], axis=0
                    )
                    for b in range(3)
                    for c in range(3)
                ],
                axis=1,
            ).astype(BF)
        )
    same = mm(jnp.concatenate(lhs, axis=0), w3_ref[1])
    first = same[0:64] + mm(lhs[1], w3_ref[2])
    second = same[64:128] + mm(lhs[0], w3_ref[0])
    out = jnp.concatenate([first[0:32], second[0:32], first[32:64], second[32:64]], axis=0)
    out = leaky(out).T
    chunk_ref[...] = out.reshape(64, 4, 128)


def finest_kernel(fin_ref, edge_ref, out_ref, wide_ref, rows_ref):
    lane = lax.broadcasted_iota(jnp.int32, (64, 128), 1)
    pair = lax.broadcasted_iota(jnp.int32, (64, 128), 0)
    for row in range(0, 8, 2):
        now = []
        for r in (row, row + 1):
            v = fin_ref[0, r].astype(F32)
            v = jnp.where(pair == 0, edge_ref[0, r, 3:4], v)
            now.append(jnp.where(pair == 63, edge_ref[0, r, 4:5], v))
        wide_ref[row // 2, pl.ds(0, 64, stride=2), :] = jnp.where(
            lane < 64, now[0], pltpu.roll(now[1], 64, 1)
        )
        wide_ref[row // 2, pl.ds(1, 64, stride=2), :] = jnp.where(
            lane < 64, pltpu.roll(now[0], 64, 1), now[1]
        )
        turned = wide_ref[row // 2].T
        rows_ref[:, row, :] = turned[0:64]
        rows_ref[:, row + 1, :] = turned[64:128]
    out_ref[:, 0] = rows_ref[...].astype(BF)


def coarse_kernel(in_ref, out_ref, y_ref):
    for c in range(4):
        v = in_ref[:, c, :]
        y_ref[pl.ds(0, 64, stride=2), :] = v
        y_ref[pl.ds(1, 64, stride=2), :] = pltpu.roll(v, 64, 1)
        out_ref[c] = y_ref[...].T[0:64].reshape(2, 32, 128).astype(BF)


def shift(array, axis, step):
    peers = lax.axis_size(axis)
    return lax.ppermute(array, axis, [(i, (i + step) % peers) for i in range(peers)])


def struct(shape, dtype):
    return jax.ShapeDtypeStruct(shape, dtype)


def on_device(disp, lift_w, conv1_w, reduce1_w, conv2_w, reduce2_w, conv3_w):
    own = disp.reshape(24, 8, 128)
    up = shift(own, "wide", 1)
    wl, w1 = call(
        fine_weights_kernel,
        (struct((4, 256, 256), BF), struct((12, 256, 256), BF)),
        (lift_w, conv1_w.reshape(9, 192, 64)),
        4,
        name="fine_weights",
        flops=10**9,
        nbytes=4 * 10**6,
    )
    again, wl = lax.optimization_barrier((own, wl))
    down = shift(again, "wide", -1)
    dt, left, right = call(
        turn_kernel,
        (struct((24, 144, 128), F32), struct((24, 8, 128), F32), struct((24, 8, 128), F32)),
        (up, own, down),
        6,
        name="columns_to_rows",
        flops=10**7,
        nbytes=2 * 10**6,
    )
    rrecv = shift(left, "narrow", -1)
    w2 = call(
        middle_weights_kernel,
        struct((12, 384, 256), BF),
        (conv2_w.reshape(9, 384, 128),),
        6,
        name="middle_weights",
        flops=10**6,
        nbytes=4 * 10**6,
    )
    again, w2 = lax.optimization_barrier((right, w2))
    lrecv = shift(again, "narrow", 1)
    wr1 = reduce1_w.reshape(512, 128)
    fin, mid = call(
        inner_kernel,
        (struct((8, 8, 64, 128), BF), struct((4, 10, 64, 128), BF)),
        (dt, wl, w1, wr1),
        24,
        scratch=(
            VMEM((2, 1536, 256), BF),
            VMEM((8, 24, 64, 256), BF),
            VMEM((8, 10, 2, 64, 128), BF),
        ),
        name="fine_inner",
        flops=8 * 10**9,
        nbytes=8 * 10**6,
    )
    edge, skip, chunk = call(
        outer_kernel,
        (struct((8, 8, 8, 128), F32), struct((4, 4, 64, 128), BF), struct((64, 4, 128), F32)),
        (
            lrecv, left, right, rrecv, wl, w1, wr1, mid, w2,
            reduce2_w.reshape(1024, 256), conv3_w.reshape(3, 2304, 256),
        ),
        32,
        scratch=(
            VMEM((24, 32, 128), F32),
            VMEM((2, 24, 16, 128), F32),
            VMEM((2, 192, 256), BF),
            VMEM((8, 24, 8, 256), F32),
            VMEM((8, 10, 2, 8, 128), F32),
            VMEM((4, 10, 8, 128), F32),
            VMEM((40, 88, 128), F32),
            VMEM((4, 10, 80, 384), BF),
            VMEM((4, 8, 80, 128), F32),
            VMEM((2, 4, 40, 256), F32),
        ),
        name="middle_and_coarse",
        flops=6 * 10**9,
        nbytes=12 * 10**6,
    )
    received = lax.all_to_all(chunk, "wide", 0, 0, tiled=True)
    finest = pl.pallas_call(
        finest_kernel,
        grid=(8,),
        out_shape=struct((64, 8, 8, 128), BF),
        in_specs=[
            pl.BlockSpec((1, 8, 64, 128), lambda p: (p, 0, 0, 0)),
            pl.BlockSpec((1, 8, 8, 128), lambda p: (p, 0, 0, 0)),
        ],
        out_specs=pl.BlockSpec((64, 1, 8, 128), lambda p: (0, p, 0, 0)),
        scratch_shapes=[VMEM((4, 128, 128), F32), VMEM((64, 8, 128), F32)],
        compiler_params=pltpu.CompilerParams(vmem_limit_bytes=6 * MIB),
        cost_estimate=pl.CostEstimate(flops=10**8, bytes_accessed=3 * 10**6, transcendentals=0),
        name="finest_layout",
    )(fin, edge)
    coarse = call(
        coarse_kernel,
        struct((4, 2, 32, 128), BF),
        (received,),
        4,
        scratch=(VMEM((128, 128), F32),),
        name="coarse_layout",
        flops=10**6,
        nbytes=2 * 10**5,
    )
    return finest, skip.transpose(3, 0, 1, 2), coarse.transpose(0, 1, 3, 2)


def solution(mesh):
    return jax.shard_map(
        on_device,
        mesh=mesh,
        in_specs=(P(None, None, "wide", "narrow"), P(), P(), P(), P(), P(), P()),
        out_specs=(
            P(None, None, "wide", "narrow"),
            P(None, None, "wide", "narrow"),
            P("wide", None, None, "narrow"),
        ),
        check_vma=False,
    )
```

time: 77.9 us -> 58.8 us (0.75)
  the two profiles are of different devices: /device:TPU:4 before, /device:TPU:1 now
where the time goes in v1:
time: 58.8 us; the launch traced here: 58.6 us
  Pallas kernels  26.3 us (45%)
  starting transfers between devices  22.3 us (38%)
  waiting for transfers between devices  7.64 us (13%)
  local copies, waits for them, and re-layouts  1.72 us (3%)
  between operations  0.74 us (1%)
    pallas_call x6, Pallas kernels, call(): pl.pallas_call(kernel, out_shape=outs, in_specs=[whole] * len(args), out_...  22 us
    ppermute x4, starting transfers between devices, shift(): lax.ppermute(array, axis, [(i, (i + step) % peers) for i in range(peers)])  14.2 us
    all_to_all x1, starting transfers between devices, on_device(): received = lax.all_to_all(chunk, 'wide', 0, 0, tiled=True)  8.02 us
    all_to_all x1, waiting for transfers between devices, on_device(): received = lax.all_to_all(chunk, 'wide', 0, 0, tiled=True)  6.31 us
    pallas_call x1, Pallas kernels, on_device(): pl.pallas_call(finest_kernel, grid=(8,), out_shape=struct((64, 8, 8, 128)...  4.31 us
    unnamed x14, local copies, waits for them, and re-layouts  1.72 us
    ppermute x4, waiting for transfers between devices, shift(): lax.ppermute(array, axis, [(i, (i + step) % peers) for i in range(peers)])  1.33 us
  transfers between devices with their start and end apart: 5, of which 2 were waited for; matrix products, arithmetic and copies ran while one was open for 0% of the time, Pallas kernels for 27%

profile of v1, /device:TPU:1, one launch (start us, length us, event | category | flops | bytes accessed | tf_op | source)
XLA Modules:
  0.0 58.6 jit_solution(15694488663834663656)
XLA Ops:
  0.6 0.0 copy-start.1
  0.6 0.0 copy-start
  0.7 2.5 %collective-permute-start = (f32[24,8,128]{2,1,0:T(8,128)}, f32[24,8,128]{2,1,0:T(8,128)S(1)}, u32[]{:S(2)}, u32[]{:S(2)}) collective-permute-start(f32[24,8,128]{2,1,0:T(8,128)} %bitcast.9), channel_id=1, source_target_pairs={{0,4},{4,8},{8,12},{12,16},{16,20},{20,24},{24,28},{28,32},{32,36}... | collective-permute-start | bytes 294920 | tf_op jit(solution)/shard_map/ppermute | solution.py:292
  3.2 1.0 %copy-done.4 = bf16[3,3,3,64,64]{4,3,2,1,0:T(8,128)(2,1)S(1)} copy-done((bf16[3,3,3,64,64]{4,3,2,1,0:T(8,128)(2,1)S(1)}, bf16[3,3,3,64,64]{4,3,2,1,0:T(8,128)(2,1)}, u32[]{:S(2)}) %copy-start.4) | copy-done | bytes 221208
  4.2 0.7 %copy-done.6 = f32[3,64]{1,0:T(4,128)S(1)} copy-done((f32[3,64]{1,0:T(4,128)S(1)}, f32[3,64]{1,0:T(4,128)}, u32[]{:S(2)}) %copy-start.6) | copy-done | bytes 792
  4.9 0.5 fine_weights.1
  5.4 0.0 copy-start.5
  5.4 0.0 copy-done.1
  5.5 7.5 %collective-permute-start.1 = (f32[24,8,128]{2,1,0:T(8,128)S(1)}, f32[24,8,128]{2,1,0:T(8,128)S(1)}, u32[]{:S(2)}, u32[]{:S(2)}) collective-permute-start(f32[24,8,128]{2,1,0:T(8,128)S(1)} %bitcast.10), channel_id=1, source_target_pairs={{0,252},{4,0},{8,4},{12,8},{16,12},{20,16},{24,20},{28,24},{32,28}... | collective-permute-start | bytes 294920 | tf_op jit(solution)/shard_map/ppermute | solution.py:292
  12.9 0.3 middle_weights.1.w2_ref
  13.2 0.0 collective-permute-done.up_ref
  13.2 1.3 %collective-permute-done.1.down_ref = f32[24,8,128]{2,1,0:T(8,128)S(1)} collective-permute-done((f32[24,8,128]{2,1,0:T(8,128)S(1)}, f32[24,8,128]{2,1,0:T(8,128)S(1)}, u32[]{:S(2)}, u32[]{:S(2)}) %collective-permute-start.1) | collective-permute-done | bytes 98336 | tf_op jit(solution)/shard_map/ppermute | solution.py:292
  14.6 0.5 columns_to_rows.1
  15.0 1.6 %collective-permute-start.3 = (f32[24,8,128]{2,1,0:T(8,128)S(1)}, f32[24,8,128]{2,1,0:T(8,128)S(1)}, u32[]{:S(2)}, u32[]{:S(2)}) collective-permute-start(f32[24,8,128]{2,1,0:T(8,128)S(1)} %get-tuple-element.25.left_ref), channel_id=1, source_target_pairs={{0,3},{1,0},{2,1},{3,2},{4,7},{5,4},{6,5},{7,6},{8,11},{9,8},{10,9... | collective-permute-start | bytes 294920 | tf_op jit(solution)/shard_map/ppermute | solution.py:292
  16.7 2.6 %collective-permute-start.2 = (f32[24,8,128]{2,1,0:T(8,128)S(1)}, f32[24,8,128]{2,1,0:T(8,128)S(1)}, u32[]{:S(2)}, u32[]{:S(2)}) collective-permute-start(f32[24,8,128]{2,1,0:T(8,128)S(1)} %get-tuple-element.24.right_ref), channel_id=1, source_target_pairs={{0,1},{1,2},{2,3},{3,0},{4,5},{5,6},{6,7},{7,4},{8,9},{9,10},{10,1... | collective-permute-start | bytes 294920 | tf_op jit(solution)/shard_map/ppermute | solution.py:292
  19.3 10.5 %fine_inner.1 = (bf16[8,8,64,128]{3,2,1,0:T(8,128)(2,1)S(1)}, bf16[4,10,64,128]{3,2,1,0:T(8,128)(2,1)S(1)}) custom-call(f32[24,144,128]{2,1,0:T(8,128)S(1)} %get-tuple-element.19.dt_ref, bf16[4,256,256]{2,1,0:T(8,128)(2,1)S(1)} %get-tuple-element.20.wl_ref, bf16[12,256,256]{2,1,0:T(8,128)(2,1)S(1)} %get-tuple-element.21.w1_ref, bf16[512,128]{1,0:T(8,128)(2,1)S(1)} %bitcast.15), custom_call_target="tpu_custom_call" | custom-call | flops 8000000000 | bytes 8000000 | tf_op jit(solution)/shard_map/fine_inner/pallas_call | solution.py:28
  29.8 0.0 collective-permute-done.3.rrecv_ref
  29.8 0.0 collective-permute-done.2.lrecv_ref
  29.8 0.0 copy-done.2
  29.8 9.2 %middle_and_coarse.1 = (f32[8,8,8,128]{3,2,1,0:T(8,128)S(1)}, bf16[4,4,64,128]{3,2,1,0:T(8,128)(2,1)}, f32[64,4,128]{2,1,0:T(4,128)}) custom-call(f32[24,8,128]{2,1,0:T(8,128)S(1)} %collective-permute-done.2.lrecv_ref, f32[24,8,128]{2,1,0:T(8,128)S(1)} %get-tuple-element.25.left_ref, f32[24,8,128]{2,1,0:T(8,128)S(1)} %get-tuple-element.24.right_ref, ...), custom_call_target="tpu_custom_call" | custom-call | flops 6000000000 | bytes 12000000 | tf_op jit(solution)/shard_map/middle_and_coarse/pallas_call | solution.py:28
  39.0 8.0 %all-to-all-start = ((f32[64,4,128]{2,1,0:T(4,128)}), f32[64,4,128]{2,1,0:T(4,128)S(1)}, u32[]{:S(2)}, u32[]{:S(2)}) async-start(f32[64,4,128]{2,1,0:T(4,128)} %get-tuple-element.30), calls=%async_computation | async-start | bytes 262144 | tf_op jit(solution)/shard_map/all_to_all | solution.py:373
  47.1 4.3 %finest_layout.1 = bf16[64,8,8,128]{3,2,1,0:T(8,128)(2,1)} custom-call(bf16[8,8,64,128]{3,2,1,0:T(8,128)(2,1)S(1)} %get-tuple-element.22.fin_ref, f32[8,8,8,128]{3,2,1,0:T(8,128)S(1)} %get-tuple-element.28.edge_ref), custom_call_target="tpu_custom_call" | custom-call | flops 100000000 | bytes 3000000 | tf_op jit(solution)/shard_map/finest_layout/pallas_call | solution.py:374
  51.4 6.3 %all-to-all-done.in_ref = f32[64,4,128]{2,1,0:T(4,128)S(1)} async-done(((f32[64,4,128]{2,1,0:T(4,128)}), f32[64,4,128]{2,1,0:T(4,128)S(1)}, u32[]{:S(2)}, u32[]{:S(2)}) %all-to-all-start) | async-done | bytes 131104 | tf_op jit(solution)/shard_map/all_to_all | solution.py:373
  57.7 0.9 %coarse_layout.1 = bf16[4,2,32,128]{3,2,1,0:T(8,128)(2,1)} custom-call(f32[64,4,128]{2,1,0:T(4,128)S(1)} %all-to-all-done.in_ref), custom_call_target="tpu_custom_call" | custom-call | flops 1000000 | bytes 200000 | tf_op jit(solution)/shard_map/coarse_layout/pallas_call | solution.py:28
  (7 shorter events, 0.0 us)
Async XLA Ops:
  0.6 4.8 %copy-start.1 = (f32[3,8,8,128]{3,2,1,0:T(8,128)S(1)}, f32[3,8,8,128]{3,2,1,0:T(8,128)}, u32[]{:S(2)}) copy-start(f32[3,8,8,128]{3,2,1,0:T(8,128)} %param.7) | copy-start | bytes 294916
  0.6 12.3 %copy-start = (bf16[3,3,3,128,128]{4,3,2,1,0:T(8,128)(2,1)S(1)}, bf16[3,3,3,128,128]{4,3,2,1,0:T(8,128)(2,1)}, u32[]{:S(2)}) copy-start(bf16[3,3,3,128,128]{4,3,2,1,0:T(8,128)(2,1)} %param.11) | copy-start | bytes 2654212
  0.7 12.6 %collective-permute-start = (f32[24,8,128]{2,1,0:T(8,128)}, f32[24,8,128]{2,1,0:T(8,128)S(1)}, u32[]{:S(2)}, u32[]{:S(2)}) collective-permute-start(f32[24,8,128]{2,1,0:T(8,128)} %bitcast.9), channel_id=1, source_target_pairs={{0,4},{4,8},{8,12},{12,16},{16,20},{20,24},{24,28},{28,32},{32,36}... | collective-permute-start | bytes 294920 | tf_op jit(solution)/shard_map/ppermute | solution.py:292
  3.2 1.0 %copy-start.4 = (bf16[3,3,3,64,64]{4,3,2,1,0:T(8,128)(2,1)S(1)}, bf16[3,3,3,64,64]{4,3,2,1,0:T(8,128)(2,1)}, u32[]{:S(2)}) copy-start(bf16[3,3,3,64,64]{4,3,2,1,0:T(8,128)(2,1)} %param.9) | copy-start | bytes 663556
  4.2 0.7 %copy-start.6 = (f32[3,64]{1,0:T(4,128)S(1)}, f32[3,64]{1,0:T(4,128)}, u32[]{:S(2)}) copy-start(f32[3,64]{1,0:T(4,128)} %lift_ref.1) | copy-start | bytes 2308
  5.4 13.8 %copy-start.5 = (bf16[2,2,2,64,128]{4,3,2,1,0:T(8,128)(2,1)S(1)}, bf16[2,2,2,64,128]{4,3,2,1,0:T(8,128)(2,1)}, u32[]{:S(2)}) copy-start(bf16[2,2,2,64,128]{4,3,2,1,0:T(8,128)(2,1)} %param.10) | copy-start | bytes 393220
  5.5 9.1 %collective-permute-start.1 = (f32[24,8,128]{2,1,0:T(8,128)S(1)}, f32[24,8,128]{2,1,0:T(8,128)S(1)}, u32[]{:S(2)}, u32[]{:S(2)}) collective-permute-start(f32[24,8,128]{2,1,0:T(8,128)S(1)} %bitcast.10), channel_id=1, source_target_pairs={{0,252},{4,0},{8,4},{12,8},{16,12},{20,16},{24,20},{28,24},{32,28}... | collective-permute-start | bytes 294920 | tf_op jit(solution)/shard_map/ppermute | solution.py:292
  15.0 14.8 %collective-permute-start.3 = (f32[24,8,128]{2,1,0:T(8,128)S(1)}, f32[24,8,128]{2,1,0:T(8,128)S(1)}, u32[]{:S(2)}, u32[]{:S(2)}) collective-permute-start(f32[24,8,128]{2,1,0:T(8,128)S(1)} %get-tuple-element.25.left_ref), channel_id=1, source_target_pairs={{0,3},{1,0},{2,1},{3,2},{4,7},{5,4},{6,5},{7,6},{8,11},{9,8},{10,9... | collective-permute-start | bytes 294920 | tf_op jit(solution)/shard_map/ppermute | solution.py:292
  16.7 13.2 %collective-permute-start.2 = (f32[24,8,128]{2,1,0:T(8,128)S(1)}, f32[24,8,128]{2,1,0:T(8,128)S(1)}, u32[]{:S(2)}, u32[]{:S(2)}) collective-permute-start(f32[24,8,128]{2,1,0:T(8,128)S(1)} %get-tuple-element.24.right_ref), channel_id=1, source_target_pairs={{0,1},{1,2},{2,3},{3,0},{4,5},{5,6},{6,7},{7,4},{8,9},{9,10},{10,1... | collective-permute-start | bytes 294920 | tf_op jit(solution)/shard_map/ppermute | solution.py:292
  19.3 10.6 %copy-start.2 = (bf16[3,3,3,256,256]{4,3,2,1,0:T(8,128)(2,1)S(1)}, bf16[3,3,3,256,256]{4,3,2,1,0:T(8,128)(2,1)}, u32[]{:S(2)}) copy-start(bf16[3,3,3,256,256]{4,3,2,1,0:T(8,128)(2,1)} %param.13) | copy-start | bytes 10616836
  19.3 10.6 %copy-start.3 = (bf16[2,2,2,128,256]{4,3,2,1,0:T(8,128)(2,1)S(1)}, bf16[2,2,2,128,256]{4,3,2,1,0:T(8,128)(2,1)}, u32[]{:S(2)}) copy-start(bf16[2,2,2,128,256]{4,3,2,1,0:T(8,128)(2,1)} %param.12) | copy-start | bytes 1572868
  39.0 18.7 %all-to-all-start = ((f32[64,4,128]{2,1,0:T(4,128)}), f32[64,4,128]{2,1,0:T(4,128)S(1)}, u32[]{:S(2)}, u32[]{:S(2)}) async-start(f32[64,4,128]{2,1,0:T(4,128)} %get-tuple-element.30), calls=%async_computation | async-start | bytes 262144 | tf_op jit(solution)/shard_map/all_to_all | solution.py:373

commit v2 on v1

--- a/solution.py
+++ b/solution.py
@@ -23,12 +23,12 @@
     return jnp.dot(a, b, preferred_element_type=F32)
 
 
-def call(kernel, outs, args, limit, scratch=(), name=None, flops=0, nbytes=0):
+def call(kernel, outs, args, limit, scratch=(), name=None, flops=0, nbytes=0, space=VMEM):
     whole = pl.BlockSpec(memory_space=VMEM)
     return pl.pallas_call(
         kernel,
         out_shape=outs,
-        in_specs=[whole] * len(args),
+        in_specs=[pl.BlockSpec(memory_space=space)] * len(args),
         out_specs=jax.tree.map(lambda _: whole, outs),
         scratch_shapes=list(scratch),
         compiler_params=pltpu.CompilerParams(vmem_limit_bytes=limit * MIB),
@@ -37,7 +37,7 @@
     )(*args)
 
 
-def fine_weights_kernel(lift_ref, c1_ref, wl_ref, w1_ref):
+def lift_weights(lift_ref, wl_ref):
     w = lift_ref[...]
     hi = rounded(w)
     low = rounded(w - hi)
@@ -60,6 +60,9 @@
         for j in range(2):
             keep = (row == 2 * t + lane // 128) & (lane // 64 % 2 == j)
             wl_ref[t, j * 128 : (j + 1) * 128, :] = jnp.where(keep, base, 0.0).astype(BF)
+
+
+def conv1_weights(c1_ref, w1_ref):
     rows64 = lax.broadcasted_iota(jnp.int32, (64, 128), 0)
     lanes64 = lax.broadcasted_iota(jnp.int32, (64, 128), 1)
     left = (rows64 == lanes64).astype(BF)
@@ -89,86 +92,166 @@
         w2_ref[b, :, 128:256] = zero2
 
 
-def turn_kernel(up_ref, own_ref, down_ref, dt_ref, left_ref, right_ref):
+def turned(src, plane):
+    parts = [[], [], []]
+    for m in range(3):
+        v = src[m * 8 + plane]
+        hi = rounded(v)
+        rest = v - hi
+        mid = rounded(rest)
+        parts[0].append(hi)
+        parts[1].append(mid)
+        parts[2].append(rest - mid)
+    tiles = parts[0] + parts[0] + parts[1] + parts[1] + parts[2]
+    tiles.append(jnp.zeros((8, 128), F32))
+    return jnp.concatenate(tiles, axis=0).T
+
+
+def turn_block(src, dt_ref, left_ref, right_ref):
     for plane in range(8):
-        for blk, src in enumerate((up_ref, own_ref, down_ref)):
-            parts = [[], [], []]
-            for m in range(3):
-                v = src[m * 8 + plane]
-                hi = rounded(v)
-                rest = v - hi
-                mid = rounded(rest)
-                parts[0].append(hi)
-                parts[1].append(mid)
-                parts[2].append(rest - mid)
-            tiles = parts[0] + parts[0] + parts[1] + parts[1] + parts[2]
-            tiles.append(jnp.zeros((8, 128), F32))
-            turned = jnp.concatenate(tiles, axis=0).T
-            g = plane * 3 + blk
-            dt_ref[g, 8:136] = turned
-            left_ref[g] = turned[0:8]
-            right_ref[g] = turned[120:128]
-    dt_ref[:, 0:8, :] = jnp.zeros((24, 8, 128), F32)
-    dt_ref[:, 136:144, :] = jnp.zeros((24, 8, 128), F32)
-
-
-def fine_levels(lhs_ref, wl_ref, w1_ref, wr1_ref, x4_ref, fn_ref, mid_ref, pairs, chunk):
-    for t in range(4):
-        for half in range(2):
-            out = leaky(mm(lhs_ref[half], wl_ref[t])).astype(BF).astype(x4_ref.dtype)
-            out = out.reshape(24, pairs, 256)
-            lanes = slice(half * 128, (half + 1) * 128)
-            for g in range(24):
-                for r in range(2):
-                    x4_ref[g // 3, (g % 3) * 8 + 2 * t + r, :, lanes] = out[
-                        g, :, r * 128 : (r + 1) * 128
-                    ]
-    for pp in range(4):
-        taps = [dp for dp in range(4) if 0 <= 2 * pp - 1 + dp < 8]
-        weight = w1_ref[taps[0] * 3 : taps[-1] * 3 + 3].reshape(len(taps) * 768, 256)
-        for r0 in range(0, 20, chunk):
-            lhs = jnp.concatenate(
-                [
-                    x4_ref[2 * pp - 1 + dp, 1 + b + r0 : 1 + b + r0 + chunk].reshape(
-                        chunk * pairs, 256
-                    )
-                    for dp in taps
-                    for b in range(3)
-                ],
-                axis=1,
-            ).astype(BF)
-            out = leaky(mm(lhs, weight)).astype(BF).astype(fn_ref.dtype)
-            for q in range(2):
-                fn_ref[2 * pp + q, r0 // 2 : (r0 + chunk) // 2] = out[
-                    :, q * 128 : (q + 1) * 128
-                ].reshape(chunk // 2, 2, pairs, 128)
-        lhs = jnp.concatenate(
-            [
-                fn_ref[2 * pp + a, :, b].reshape(10 * pairs, 128)
-                for a in range(2)
-                for b in range(2)
-            ],
-            axis=1,
-        ).astype(BF)
-        out = leaky(mm(lhs, wr1_ref[...])).astype(BF)
-        mid_ref[pp] = out.astype(mid_ref.dtype).reshape(10, pairs, 128)
-
-
-def inner_kernel(dt_ref, wl_ref, w1_ref, wr1_ref, fin_ref, mid_ref, lhs_ref, x4_ref, fn_ref):
-    for g in range(24):
+        out = turned(src, plane)
+        dt_ref[plane, 8:136] = out
+        left_ref[plane] = out[0:8]
+        right_ref[plane] = out[120:128]
+    dt_ref[:, 0:8, :] = jnp.zeros((8, 8, 128), F32)
+    dt_ref[:, 136:144, :] = jnp.zeros((8, 8, 128), F32)
+
+
+def turn_kernel(down_ref, lup_ref, rup_ref, lown_ref, rown_ref, dt_ref, left_ref, right_ref):
+    turn_block(down_ref, dt_ref, left_ref.at[16:24], right_ref.at[16:24])
+    left_ref[0:8] = lup_ref[...]
+    right_ref[0:8] = rup_ref[...]
+    left_ref[8:16] = lown_ref[...]
+    right_ref[8:16] = rown_ref[...]
+
+
+def window_columns(dt_ref, lhs_ref, groups):
+    for g in range(groups):
         for half in range(2):
             lhs_ref[half, g * 64 : (g + 1) * 64, :] = jnp.concatenate(
                 [dt_ref[g, pl.ds(7 + 2 * half + j, 64, stride=2)] for j in range(2)], axis=1
             ).astype(BF)
-    fine_levels(lhs_ref, wl_ref, w1_ref, wr1_ref, x4_ref, fn_ref, mid_ref, 64, 10)
+
+
+def lift(lhs_ref, wl_ref, groups, pairs, dtype, store):
+    for t in range(4):
+        for half in range(2):
+            out = leaky(mm(lhs_ref[half], wl_ref[t])).astype(BF).astype(dtype)
+            out = out.reshape(groups, pairs, 256)
+            for g in range(groups):
+                for r in range(2):
+                    store(
+                        g,
+                        2 * t + r,
+                        slice(half * 128, (half + 1) * 128),
+                        out[g, :, r * 128 : (r + 1) * 128],
+                    )
+
+
+def conv1(lhs_of, w1_ref, pp):
+    taps = [dp for dp in range(4) if 0 <= 2 * pp - 1 + dp < 8]
+    weight = w1_ref[taps[0] * 3 : taps[-1] * 3 + 3].reshape(len(taps) * 768, 256)
+    lhs = jnp.concatenate(
+        [lhs_of(2 * pp - 1 + dp, b) for dp in taps for b in range(3)], axis=1
+    ).astype(BF)
+    return leaky(mm(lhs, weight)).astype(BF)
+
+
+def reduce1(row_of, wr1_ref):
+    lhs = jnp.concatenate(
+        [
+            jnp.concatenate([row_of(a, 2 * rr + b) for rr in range(10)], axis=0)
+            for a in range(2)
+            for b in range(2)
+        ],
+        axis=1,
+    ).astype(BF)
+    return leaky(mm(lhs, wr1_ref[...])).astype(BF)
+
+
+def put_planes(out, pp, rows, fn_ref):
+    for q in range(2):
+        fn_ref[2 * pp + q] = out[:, q * 128 : (q + 1) * 128].reshape(rows, 64, 128)
+
+
+def own_kernel(
+    own_hbm, lift_hbm, c1_hbm, x4b_ref, fn_ref, lown_ref, rown_ref, wl_ref, w1_ref,
+    dt_ref, lhs_ref, x4_ref, own_ref, lift_ref, c1_ref, sems,
+):
+    copies = [
+        pltpu.make_async_copy(src, dst, sems.at[n])
+        for n, (src, dst) in enumerate(
+            ((own_hbm, own_ref), (lift_hbm, lift_ref), (c1_hbm, c1_ref))
+        )
+    ]
+    for copy in copies:
+        copy.start()
+    copies[0].wait()
+    turn_block(own_ref, dt_ref, lown_ref, rown_ref)
+    copies[1].wait()
+    lift_weights(lift_ref, wl_ref)
+    copies[2].wait()
+    conv1_weights(c1_ref, w1_ref)
+    window_columns(dt_ref, lhs_ref, 8)
+
+    def store(g, row, lanes, values):
+        x4_ref[g, row, :, lanes] = values
+        if row in (0, 1, 6, 7):
+            x4b_ref[g, row if row < 2 else row - 4, :, lanes] = values
+
+    lift(lhs_ref, wl_ref, 8, 64, BF, store)
+    for pp in range(4):
+        out = conv1(lambda plane, b: x4_ref[plane, b : b + 6].reshape(384, 256), w1_ref, pp)
+        put_planes(out, pp, 6, fn_ref)
+
+
+def top_kernel(up_ref, x4b_ref, wl_ref, w1_ref, fn_ref, lup_ref, rup_ref, dt_ref, lhs_ref, x4_ref):
+    turn_block(up_ref, dt_ref, lup_ref, rup_ref)
+    window_columns(dt_ref, lhs_ref, 8)
+
+    def store(g, row, lanes, values):
+        x4_ref[g, row, :, lanes] = values
+
+    lift(lhs_ref, wl_ref, 8, 64, BF, store)
     for plane in range(8):
-        fin_ref[plane] = fn_ref[plane, 3:7].reshape(8, 64, 128)
+        x4_ref[plane, 8:10] = x4b_ref[plane, 0:2]
+    for pp in range(4):
+        out = conv1(
+            lambda plane, b: x4_ref[plane, 1 + b : 8 + b].reshape(448, 256), w1_ref, pp
+        )
+        put_planes(out, pp, 7, fn_ref)
+
+
+def bottom_kernel(
+    dt_ref, x4b_ref, fnt_ref, fno_ref, wl_ref, w1_ref, wr1_ref, fn_ref, mid_ref, lhs_ref, x4_ref
+):
+    window_columns(dt_ref, lhs_ref, 8)
+
+    def store(g, row, lanes, values):
+        x4_ref[g, row + 2, :, lanes] = values
+
+    lift(lhs_ref, wl_ref, 8, 64, BF, store)
+    for plane in range(8):
+        x4_ref[plane, 0:2] = x4b_ref[plane, 2:4]
+    for pp in range(4):
+        out = conv1(lambda plane, b: x4_ref[plane, b : b + 7].reshape(448, 256), w1_ref, pp)
+        put_planes(out, pp, 7, fn_ref)
+    for pp in range(4):
+
+        def row_of(a, row):
+            if row < 7:
+                return fnt_ref[2 * pp + a, row]
+            if row < 13:
+                return fno_ref[2 * pp + a, row - 7]
+            return fn_ref[2 * pp + a, row - 13]
+
+        mid_ref[pp] = reduce1(row_of, wr1_ref).reshape(10, 64, 128)
 
 
 def outer_kernel(
     lrecv_ref, left_ref, right_ref, rrecv_ref, wl_ref, w1_ref, wr1_ref, main_ref, w2_ref, wr2_ref, w3_ref,
-    edge_ref, skip_ref, chunk_ref,
-    de_ref, dw_ref, lhs_ref, x4_ref, fn_ref, me_ref, mf_ref, xm_ref, ms_ref, cf_ref,
+    fn_ref, skip_ref, chunk_ref,
+    de_ref, dw_ref, lhs_ref, x4_ref, me_ref, mf_ref, xm_ref, ms_ref, cf_ref,
 ):
     de_ref[:, 0:8] = lrecv_ref[...]
     de_ref[:, 8:16] = left_ref[...]
@@ -188,9 +271,19 @@
                 ],
                 axis=1,
             ).astype(BF)
-    fine_levels(lhs_ref, wl_ref, w1_ref, wr1_ref, x4_ref, fn_ref, me_ref, 8, 20)
-    for plane in range(8):
-        edge_ref[plane] = fn_ref[plane, 3:7].reshape(8, 8, 128)
+
+    def store(g, row, lanes, values):
+        x4_ref[g % 8, g // 8 * 8 + row, :, lanes] = values
+
+    lift(lhs_ref, wl_ref, 24, 8, F32, store)
+    for pp in range(4):
+        out = conv1(
+            lambda plane, b: x4_ref[plane, 1 + b : 21 + b].reshape(160, 256), w1_ref, pp
+        ).astype(F32)
+        for q in range(2):
+            fn_ref[2 * pp + q] = out[:, q * 128 : (q + 1) * 128].reshape(20, 8, 128)
+        mid = reduce1(lambda a, row: fn_ref[2 * pp + a, row], wr1_ref)
+        me_ref[pp] = mid.astype(F32).reshape(10, 8, 128)
 
     def merge(n, carry):
         plane, row = n // 10, n % 10
@@ -255,18 +348,18 @@
     second = same[64:128] + mm(lhs[0], w3_ref[0])
     out = jnp.concatenate([first[0:32], second[0:32], first[32:64], second[32:64]], axis=0)
     out = leaky(out).T
-    chunk_ref[...] = out.reshape(64, 4, 128)
-
-
-def finest_kernel(fin_ref, edge_ref, out_ref, wide_ref, rows_ref):
+    chunk_ref[...] = out.reshape(64, 4, 128).astype(BF)
+
+
+def finest_kernel(fnt_ref, fno_ref, fnb_ref, edge_ref, out_ref, wide_ref, rows_ref):
     lane = lax.broadcasted_iota(jnp.int32, (64, 128), 1)
     pair = lax.broadcasted_iota(jnp.int32, (64, 128), 0)
     for row in range(0, 8, 2):
         now = []
         for r in (row, row + 1):
-            v = fin_ref[0, r].astype(F32)
-            v = jnp.where(pair == 0, edge_ref[0, r, 3:4], v)
-            now.append(jnp.where(pair == 63, edge_ref[0, r, 4:5], v))
+            v = (fnt_ref[0, 0] if r == 0 else fnb_ref[0, 0] if r == 7 else fno_ref[0, r - 1]).astype(F32)
+            v = jnp.where(pair == 0, edge_ref[0, r + 6, 3:4], v)
+            now.append(jnp.where(pair == 63, edge_ref[0, r + 6, 4:5], v))
         wide_ref[row // 2, pl.ds(0, 64, stride=2), :] = jnp.where(
             lane < 64, now[0], pltpu.roll(now[1], 64, 1)
         )
@@ -280,8 +373,9 @@
 
 
 def coarse_kernel(in_ref, out_ref, y_ref):
+    all_in = in_ref[...].astype(F32)
     for c in range(4):
-        v = in_ref[:, c, :]
+        v = all_in[:, c, :]
         y_ref[pl.ds(0, 64, stride=2), :] = v
         y_ref[pl.ds(1, 64, stride=2), :] = pltpu.roll(v, 64, 1)
         out_ref[c] = y_ref[...].T[0:64].reshape(2, 32, 128).astype(BF)
@@ -299,27 +393,37 @@
 def on_device(disp, lift_w, conv1_w, reduce1_w, conv2_w, reduce2_w, conv3_w):
     own = disp.reshape(24, 8, 128)
     up = shift(own, "wide", 1)
-    wl, w1 = call(
-        fine_weights_kernel,
-        (struct((4, 256, 256), BF), struct((12, 256, 256), BF)),
-        (lift_w, conv1_w.reshape(9, 192, 64)),
-        4,
-        name="fine_weights",
-        flops=10**9,
-        nbytes=4 * 10**6,
-    )
-    again, wl = lax.optimization_barrier((own, wl))
+    strip = struct((8, 8, 128), F32)
+    fine_scratch = (VMEM((2, 512, 256), BF), VMEM((8, 10, 64, 256), BF))
+    turn_scratch = (VMEM((8, 144, 128), F32),)
+    stay = lambda x: pltpu.with_memory_space_constraint(x, pltpu.HBM)
+    x4b, fno, lown, rown, wl, w1 = call(
+        own_kernel,
+        (
+            struct((8, 4, 64, 256), BF),
+            struct((8, 6, 64, 128), BF),
+            strip,
+            strip,
+            struct((4, 256, 256), BF),
+            struct((12, 256, 256), BF),
+        ),
+        (stay(own), stay(lift_w), stay(conv1_w.reshape(9, 192, 64))),
+        14,
+        scratch=turn_scratch
+        + fine_scratch
+        + (
+            VMEM((24, 8, 128), F32),
+            VMEM((3, 64), F32),
+            VMEM((9, 192, 64), BF),
+            pltpu.SemaphoreType.DMA((3,)),
+        ),
+        name="fine_own_rows",
+        flops=2 * 10**9,
+        nbytes=6 * 10**6,
+        space=pltpu.HBM,
+    )
+    again, x4b = lax.optimization_barrier((own, x4b))
     down = shift(again, "wide", -1)
-    dt, left, right = call(
-        turn_kernel,
-        (struct((24, 144, 128), F32), struct((24, 8, 128), F32), struct((24, 8, 128), F32)),
-        (up, own, down),
-        6,
-        name="columns_to_rows",
-        flops=10**7,
-        nbytes=2 * 10**6,
-    )
-    rrecv = shift(left, "narrow", -1)
     w2 = call(
         middle_weights_kernel,
         struct((12, 384, 256), BF),
@@ -329,37 +433,51 @@
         flops=10**6,
         nbytes=4 * 10**6,
     )
-    again, w2 = lax.optimization_barrier((right, w2))
-    lrecv = shift(again, "narrow", 1)
+    fnt, lup, rup = call(
+        top_kernel,
+        (struct((8, 7, 64, 128), BF), strip, strip),
+        (up, x4b, wl, w1),
+        12,
+        scratch=turn_scratch + fine_scratch,
+        name="fine_top_rows",
+        flops=3 * 10**9,
+        nbytes=6 * 10**6,
+    )
+    dt, left, right = call(
+        turn_kernel,
+        (struct((8, 144, 128), F32), struct((24, 8, 128), F32), struct((24, 8, 128), F32)),
+        (down, lup, rup, lown, rown),
+        6,
+        name="columns_to_rows",
+        flops=10**7,
+        nbytes=2 * 10**6,
+    )
+    rrecv = shift(left, "narrow", -1)
+    lrecv = shift(right, "narrow", 1)
     wr1 = reduce1_w.reshape(512, 128)
-    fin, mid = call(
-        inner_kernel,
-        (struct((8, 8, 64, 128), BF), struct((4, 10, 64, 128), BF)),
-        (dt, wl, w1, wr1),
-        24,
-        scratch=(
-            VMEM((2, 1536, 256), BF),
-            VMEM((8, 24, 64, 256), BF),
-            VMEM((8, 10, 2, 64, 128), BF),
-        ),
-        name="fine_inner",
+    fnb, mid = call(
+        bottom_kernel,
+        (struct((8, 7, 64, 128), BF), struct((4, 10, 64, 128), BF)),
+        (dt, x4b, fnt, fno, wl, w1, wr1),
+        14,
+        scratch=fine_scratch,
+        name="fine_bottom_rows",
         flops=8 * 10**9,
-        nbytes=8 * 10**6,
+        nbytes=6 * 10**6,
     )
     edge, skip, chunk = call(
         outer_kernel,
-        (struct((8, 8, 8, 128), F32), struct((4, 4, 64, 128), BF), struct((64, 4, 128), F32)),
+        (struct((8, 20, 8, 128), F32), struct((4, 4, 64, 128), BF), struct((64, 4, 128), BF)),
         (
             lrecv, left, right, rrecv, wl, w1, wr1, mid, w2,
             reduce2_w.reshape(1024, 256), conv3_w.reshape(3, 2304, 256),
         ),
-        32,
+        24,
         scratch=(
             VMEM((24, 32, 128), F32),
             VMEM((2, 24, 16, 128), F32),
             VMEM((2, 192, 256), BF),
             VMEM((8, 24, 8, 256), F32),
-            VMEM((8, 10, 2, 8, 128), F32),
             VMEM((4, 10, 8, 128), F32),
             VMEM((40, 88, 128), F32),
             VMEM((4, 10, 80, 384), BF),
@@ -376,15 +494,17 @@
         grid=(8,),
         out_shape=struct((64, 8, 8, 128), BF),
         in_specs=[
-            pl.BlockSpec((1, 8, 64, 128), lambda p: (p, 0, 0, 0)),
-            pl.BlockSpec((1, 8, 8, 128), lambda p: (p, 0, 0, 0)),
+            pl.BlockSpec((1, 1, 64, 128), lambda p: (p, 6, 0, 0)),
+            pl.BlockSpec((1, 6, 64, 128), lambda p: (p, 0, 0, 0)),
+            pl.BlockSpec((1, 1, 64, 128), lambda p: (p, 0, 0, 0)),
+            pl.BlockSpec((1, 20, 8, 128), lambda p: (p, 0, 0, 0)),
         ],
         out_specs=pl.BlockSpec((64, 1, 8, 128), lambda p: (0, p, 0, 0)),
         scratch_shapes=[VMEM((4, 128, 128), F32), VMEM((64, 8, 128), F32)],
         compiler_params=pltpu.CompilerParams(vmem_limit_bytes=6 * MIB),
         cost_estimate=pl.CostEstimate(flops=10**8, bytes_accessed=3 * 10**6, transcendentals=0),
         name="finest_layout",
-    )(fin, edge)
+    )(fnt, fno, fnb, edge)
     coarse = call(
         coarse_kernel,
         struct((4, 2, 32, 128), BF),

time: 58.8 us -> 54.5 us (0.927)
  starting transfers between devices: 22.3 us -> 19.9 us
  local copies, waits for them, and re-layouts: 1.72 us -> 0.02 us
    unnamed x14 -> x10, local copies, waits for them, and re-layouts: 1.72 us -> 0.02 us
    all_to_all x1, starting transfers between devices: 8.02 us -> 6.59 us  [on_device(): received = lax.all_to_all(chunk, 'wide', 0, 0, tiled=True)]
    ppermute x4, starting transfers between devices: 14.2 us -> 13.3 us  [shift(): lax.ppermute(array, axis, [(i, (i + step) % peers) for i in range(peers)])]
    all_to_all x1, waiting for transfers between devices: 6.31 us -> 5.47 us  [on_device(): received = lax.all_to_all(chunk, 'wide', 0, 0, tiled=True)]
    pallas_call x6 -> x7, Pallas kernels: 22 us -> 22.2 us  [call(): pl.pallas_call(kernel, out_shape=outs, in_specs=[pl.BlockSpec(memory_spac...]
  transfers between devices with their start and end apart: 5 -> 5, of which waited for: 2 -> 2; matrix products, arithmetic and copies ran while one was open for 0% -> 0% of each run, Pallas kernels for 27% -> 30%
where the time goes in v2:
time: 54.5 us; the launch traced here: 54.3 us
  Pallas kernels  26.5 us (49%)
  starting transfers between devices  19.9 us (37%)
  waiting for transfers between devices  7.11 us (13%)
  between operations  0.73 us (1%)
    pallas_call x7, Pallas kernels, call(): pl.pallas_call(kernel, out_shape=outs, in_specs=[pl.BlockSpec(memory_spac...  22.2 us
    ppermute x4, starting transfers between devices, shift(): lax.ppermute(array, axis, [(i, (i + step) % peers) for i in range(peers)])  13.3 us
    all_to_all x1, starting transfers between devices, on_device(): received = lax.all_to_all(chunk, 'wide', 0, 0, tiled=True)  6.59 us
    all_to_all x1, waiting for transfers between devices, on_device(): received = lax.all_to_all(chunk, 'wide', 0, 0, tiled=True)  5.47 us
    pallas_call x1, Pallas kernels, on_device(): pl.pallas_call(finest_kernel, grid=(8,), out_shape=struct((64, 8, 8, 128)...  4.31 us
    ppermute x4, waiting for transfers between devices, shift(): lax.ppermute(array, axis, [(i, (i + step) % peers) for i in range(peers)])  1.64 us
  transfers between devices with their start and end apart: 5, of which 2 were waited for; matrix products, arithmetic and copies ran while one was open for 0% of the time, Pallas kernels for 30%

profile of v2, /device:TPU:1, one launch (start us, length us, event | category | flops | bytes accessed | tf_op | source)
XLA Modules:
  0.0 54.3 jit_solution(201932165765434623)
XLA Ops:
  0.6 2.5 %collective-permute-start = (f32[24,8,128]{2,1,0:T(8,128)}, f32[24,8,128]{2,1,0:T(8,128)S(1)}, u32[]{:S(2)}, u32[]{:S(2)}) collective-permute-start(f32[24,8,128]{2,1,0:T(8,128)} %bitcast.15), channel_id=1, source_target_pairs={{0,4},{4,8},{8,12},{12,16},{16,20},{20,24},{24,28},{28,32},{32,36}... | collective-permute-start | bytes 294920 | tf_op jit(solution)/shard_map/ppermute | solution.py:386
  3.2 4.7 %fine_own_rows.1 = (bf16[8,4,64,256]{3,2,1,0:T(8,128)(2,1)S(1)}, bf16[8,6,64,128]{3,2,1,0:T(8,128)(2,1)S(1)}, f32[8,8,128]{2,1,0:T(8,128)S(1)}, f32[8,8,128]{2,1...) custom-call(f32[24,8,128]{2,1,0:T(8,128)} %bitcast.16, f32[3,64]{1,0:T(4,128)} %lift_hbm.1, ...), custom_call_target="tpu_custom_call" | custom-call | flops 2000000000 | bytes 6000000 | tf_op jit(solution)/shard_map/fine_own_rows/pallas_call | solution.py:28
  7.9 0.0 copy-done.4
  7.9 7.4 %collective-permute-start.1 = (f32[24,8,128]{2,1,0:T(8,128)S(1)}, f32[24,8,128]{2,1,0:T(8,128)S(1)}, u32[]{:S(2)}, u32[]{:S(2)}) collective-permute-start(f32[24,8,128]{2,1,0:T(8,128)S(1)} %bitcast.17), channel_id=1, source_target_pairs={{0,252},{4,0},{8,4},{12,8},{16,12},{20,16},{24,20},{28,24},{32,28}... | collective-permute-start | bytes 294920 | tf_op jit(solution)/shard_map/ppermute | solution.py:386
  15.3 0.0 copy-done
  15.3 0.3 middle_weights.1.w2_ref
  15.6 0.0 collective-permute-done.up_ref
  15.6 0.0 copy-start.3
  15.6 3.3 %fine_top_rows.1 = (bf16[8,7,64,128]{3,2,1,0:T(8,128)(2,1)S(1)}, f32[8,8,128]{2,1,0:T(8,128)S(1)}, f32[8,8,128]{2,1,0:T(8,128)S(1)}) custom-call(f32[24,8,128]{2,1,0:T(8,128)S(1)} %collective-permute-done.up_ref, bf16[8,4,64,256]{3,2,1,0:T(8,128)(2,1)S(1)} %get-tuple-element.23.x4b_ref, bf16[4,256,256]{2,1,0:T(8,128)(2,1)S(1)} %get-tuple-element.24.wl_ref, ...), custom_call_target="tpu_custom_call" | custom-call | flops 3000000000 | bytes 6000000 | tf_op jit(solution)/shard_map/fine_top_rows/pallas_call | solution.py:28
  18.9 0.0 collective-permute-done.1.down_ref
  18.9 0.2 columns_to_rows.1
  19.1 3.4 %collective-permute-start.2 = (f32[24,8,128]{2,1,0:T(8,128)S(1)}, f32[24,8,128]{2,1,0:T(8,128)S(1)}, u32[]{:S(2)}, u32[]{:S(2)}) collective-permute-start(f32[24,8,128]{2,1,0:T(8,128)S(1)} %get-tuple-element.35.right_ref), channel_id=1, source_target_pairs={{0,1},{1,2},{2,3},{3,0},{4,5},{5,6},{6,7},{7,4},{8,9},{9,10},{10,1... | collective-permute-start | bytes 294920 | tf_op jit(solution)/shard_map/ppermute | solution.py:386
  22.5 0.0 collective-permute-start.3
  22.5 0.0 copy-done.3
  22.5 0.0 copy-start.2
  22.5 3.9 %fine_bottom_rows.1 = (bf16[8,7,64,128]{3,2,1,0:T(8,128)(2,1)S(1)}, bf16[4,10,64,128]{3,2,1,0:T(8,128)(2,1)S(1)}) custom-call(f32[8,144,128]{2,1,0:T(8,128)S(1)} %get-tuple-element.33.dt_ref, bf16[8,4,64,256]{3,2,1,0:T(8,128)(2,1)S(1)} %get-tuple-element.23.x4b_ref, bf16[8,7,64,128]{3,2,1,0:T(8,128)(2,1)S(1)} %get-tuple-element.26.fnt_ref, ...), custom_call_target="tpu_custom_call" | custom-call | flops 8000000000 | bytes 6000000 | tf_op jit(solution)/shard_map/fine_bottom_rows/pallas_call | solution.py:28
  26.4 0.0 collective-permute-done.2.lrecv_ref
  26.4 1.6 %collective-permute-done.3.rrecv_ref = f32[24,8,128]{2,1,0:T(8,128)S(1)} collective-permute-done((f32[24,8,128]{2,1,0:T(8,128)S(1)}, f32[24,8,128]{2,1,0:T(8,128)S(1)}, u32[]{:S(2)}, u32[]{:S(2)}) %collective-permute-start.3) | collective-permute-done | bytes 98336 | tf_op jit(solution)/shard_map/ppermute | solution.py:386
  28.0 0.0 copy-done.1
  28.0 9.0 %middle_and_coarse.1 = (f32[8,20,8,128]{3,2,1,0:T(8,128)S(1)}, bf16[4,4,64,128]{3,2,1,0:T(8,128)(2,1)}, bf16[64,4,128]{2,1,0:T(4,128)(2,1)}) custom-call(f32[24,8,128]{2,1,0:T(8,128)S(1)} %collective-permute-done.2.lrecv_ref, f32[24,8,128]{2,1,0:T(8,128)S(1)} %get-tuple-element.36.left_ref, f32[24,8,128]{2,1,0:T(8,128)S(1)} %get-tuple-element.35.right_ref, ...), custom_call_target="tpu_custom_call" | custom-call | flops 6000000000 | bytes 12000000 | tf_op jit(solution)/shard_map/middle_and_coarse/pallas_call | solution.py:28
  37.0 6.6 %all-to-all-start = ((bf16[64,4,128]{2,1,0:T(4,128)(2,1)}), bf16[64,4,128]{2,1,0:T(4,128)(2,1)S(1)}, u32[]{:S(2)}, u32[]{:S(2)}) async-start(bf16[64,4,128]{2,1,0:T(4,128)(2,1)} %get-tuple-element.40), calls=%async_computation | async-start | bytes 131072 | tf_op jit(solution)/shard_map/all_to_all | solution.py:491
  43.6 4.3 %finest_layout.1 = bf16[64,8,8,128]{3,2,1,0:T(8,128)(2,1)} custom-call(bf16[8,7,64,128]{3,2,1,0:T(8,128)(2,1)S(1)} %get-tuple-element.26.fnt_ref, bf16[8,6,64,128]{3,2,1,0:T(8,128)(2,1)S(1)} %get-tuple-element.27.fno_ref, bf16[8,7,64,128]{3,2,1,0:T(8,128)(2,1)S(1)} %get-tuple-element.34.fnb_ref, f32[8,20,8,128]{3,2,1,0:T(8,128)S(1)} %get-tuple-element.38.edge_ref), custom_call_target="tpu_custom_call" | custom-call | flops 100000000 | bytes 3000000 | tf_op jit(solution)/shard_map/finest_layout/pallas_call | solution.py:492
  47.9 5.5 %all-to-all-done.in_ref = bf16[64,4,128]{2,1,0:T(4,128)(2,1)S(1)} async-done(((bf16[64,4,128]{2,1,0:T(4,128)(2,1)}), bf16[64,4,128]{2,1,0:T(4,128)(2,1)S(1)}, u32[]{:S(2)}, u32[]{:S(2)}) %all-to-all-start) | async-done | bytes 65568 | tf_op jit(solution)/shard_map/all_to_all | solution.py:491
  53.4 0.9 %coarse_layout.1 = bf16[4,2,32,128]{3,2,1,0:T(8,128)(2,1)} custom-call(bf16[64,4,128]{2,1,0:T(4,128)(2,1)S(1)} %all-to-all-done.in_ref), custom_call_target="tpu_custom_call" | custom-call | flops 1000000 | bytes 200000 | tf_op jit(solution)/shard_map/coarse_layout/pallas_call | solution.py:28
  (4 shorter events, 0.0 us)
Async XLA Ops:
  0.6 14.9 %collective-permute-start = (f32[24,8,128]{2,1,0:T(8,128)}, f32[24,8,128]{2,1,0:T(8,128)S(1)}, u32[]{:S(2)}, u32[]{:S(2)}) collective-permute-start(f32[24,8,128]{2,1,0:T(8,128)} %bitcast.15), channel_id=1, source_target_pairs={{0,4},{4,8},{8,12},{12,16},{16,20},{20,24},{24,28},{28,32},{32,36}... | collective-permute-start | bytes 294920 | tf_op jit(solution)/shard_map/ppermute | solution.py:386
  3.2 4.7 %copy-start.4 = (f32[3,8,8,128]{3,2,1,0:T(8,128)S(1)}, f32[3,8,8,128]{3,2,1,0:T(8,128)}, u32[]{:S(2)}) copy-start(f32[3,8,8,128]{3,2,1,0:T(8,128)} %param.7) | copy-start | bytes 294916
  3.2 12.1 %copy-start = (bf16[3,3,3,128,128]{4,3,2,1,0:T(8,128)(2,1)S(1)}, bf16[3,3,3,128,128]{4,3,2,1,0:T(8,128)(2,1)}, u32[]{:S(2)}) copy-start(bf16[3,3,3,128,128]{4,3,2,1,0:T(8,128)(2,1)} %param.11) | copy-start | bytes 2654212
  7.9 11.0 %collective-permute-start.1 = (f32[24,8,128]{2,1,0:T(8,128)S(1)}, f32[24,8,128]{2,1,0:T(8,128)S(1)}, u32[]{:S(2)}, u32[]{:S(2)}) collective-permute-start(f32[24,8,128]{2,1,0:T(8,128)S(1)} %bitcast.17), channel_id=1, source_target_pairs={{0,252},{4,0},{8,4},{12,8},{16,12},{20,16},{24,20},{28,24},{32,28}... | collective-permute-start | bytes 294920 | tf_op jit(solution)/shard_map/ppermute | solution.py:386
  15.6 6.9 %copy-start.3 = (bf16[2,2,2,64,128]{4,3,2,1,0:T(8,128)(2,1)S(1)}, bf16[2,2,2,64,128]{4,3,2,1,0:T(8,128)(2,1)}, u32[]{:S(2)}) copy-start(bf16[2,2,2,64,128]{4,3,2,1,0:T(8,128)(2,1)} %param.10) | copy-start | bytes 393220
  19.1 7.3 %collective-permute-start.2 = (f32[24,8,128]{2,1,0:T(8,128)S(1)}, f32[24,8,128]{2,1,0:T(8,128)S(1)}, u32[]{:S(2)}, u32[]{:S(2)}) collective-permute-start(f32[24,8,128]{2,1,0:T(8,128)S(1)} %get-tuple-element.35.right_ref), channel_id=1, source_target_pairs={{0,1},{1,2},{2,3},{3,0},{4,5},{5,6},{6,7},{7,4},{8,9},{9,10},{10,1... | collective-permute-start | bytes 294920 | tf_op jit(solution)/shard_map/ppermute | solution.py:386
  22.5 5.5 %collective-permute-start.3 = (f32[24,8,128]{2,1,0:T(8,128)S(1)}, f32[24,8,128]{2,1,0:T(8,128)S(1)}, u32[]{:S(2)}, u32[]{:S(2)}) collective-permute-start(f32[24,8,128]{2,1,0:T(8,128)S(1)} %get-tuple-element.36.left_ref), channel_id=1, source_target_pairs={{0,3},{1,0},{2,1},{3,2},{4,7},{5,4},{6,5},{7,6},{8,11},{9,8},{10,9... | collective-permute-start | bytes 294920 | tf_op jit(solution)/shard_map/ppermute | solution.py:386
  22.5 5.5 %copy-start.1 = (bf16[3,3,3,256,256]{4,3,2,1,0:T(8,128)(2,1)S(1)}, bf16[3,3,3,256,256]{4,3,2,1,0:T(8,128)(2,1)}, u32[]{:S(2)}) copy-start(bf16[3,3,3,256,256]{4,3,2,1,0:T(8,128)(2,1)} %param.13) | copy-start | bytes 10616836
  22.5 5.5 %copy-start.2 = (bf16[2,2,2,128,256]{4,3,2,1,0:T(8,128)(2,1)S(1)}, bf16[2,2,2,128,256]{4,3,2,1,0:T(8,128)(2,1)}, u32[]{:S(2)}) copy-start(bf16[2,2,2,128,256]{4,3,2,1,0:T(8,128)(2,1)} %param.12) | copy-start | bytes 1572868
  37.0 16.4 %all-to-all-start = ((bf16[64,4,128]{2,1,0:T(4,128)(2,1)}), bf16[64,4,128]{2,1,0:T(4,128)(2,1)S(1)}, u32[]{:S(2)}, u32[]{:S(2)}) async-start(bf16[64,4,128]{2,1,0:T(4,128)(2,1)} %get-tuple-element.40), calls=%async_computation | async-start | bytes 131072 | tf_op jit(solution)/shard_map/all_to_all | solution.py:491

commit v3 on v2

--- a/solution.py
+++ b/solution.py
@@ -23,12 +23,13 @@
     return jnp.dot(a, b, preferred_element_type=F32)
 
 
-def call(kernel, outs, args, limit, scratch=(), name=None, flops=0, nbytes=0, space=VMEM):
+def call(kernel, outs, args, limit, scratch=(), name=None, flops=0, nbytes=0, space=VMEM, last=None):
     whole = pl.BlockSpec(memory_space=VMEM)
     return pl.pallas_call(
         kernel,
         out_shape=outs,
-        in_specs=[pl.BlockSpec(memory_space=space)] * len(args),
+        in_specs=[pl.BlockSpec(memory_space=space)] * (len(args) - 1)
+        + [pl.BlockSpec(memory_space=last or space)],
         out_specs=jax.tree.map(lambda _: whole, outs),
         scratch_shapes=list(scratch),
         compiler_params=pltpu.CompilerParams(vmem_limit_bytes=limit * MIB),
@@ -82,16 +83,6 @@
         w1_ref[b, :, 128:256] = zero1
 
 
-def middle_weights_kernel(c2_ref, w2_ref):
-    zero2 = jnp.zeros((384, 128), BF)
-    for b in range(3):
-        for a in range(3):
-            w2_ref[a * 3 + b, :, 0:128] = c2_ref[a * 3 + b]
-            w2_ref[(a + 1) * 3 + b, :, 128:256] = c2_ref[a * 3 + b]
-        w2_ref[9 + b, :, 0:128] = zero2
-        w2_ref[b, :, 128:256] = zero2
-
-
 def turned(src, plane):
     parts = [[], [], []]
     for m in range(3):
@@ -148,30 +139,38 @@
                     )
 
 
-def conv1(lhs_of, w1_ref, pp):
-    taps = [dp for dp in range(4) if 0 <= 2 * pp - 1 + dp < 8]
+PAIRS = (
+    (0, 1, (1, 2, 3)),
+    (1, 1, (0, 1, 2, 3)),
+    (2, 1, (0, 1, 2, 3)),
+    (3, 1, (0, 1, 2)),
+)
+
+
+def conv1(lhs_of, w1_ref, taps):
     weight = w1_ref[taps[0] * 3 : taps[-1] * 3 + 3].reshape(len(taps) * 768, 256)
     lhs = jnp.concatenate(
-        [lhs_of(2 * pp - 1 + dp, b) for dp in taps for b in range(3)], axis=1
+        [lhs_of((dp - 1) // 2, (dp + 1) % 2, b) for dp in taps for b in range(3)], axis=1
     ).astype(BF)
     return leaky(mm(lhs, weight)).astype(BF)
 
 
-def reduce1(row_of, wr1_ref):
-    lhs = jnp.concatenate(
-        [
-            jnp.concatenate([row_of(a, 2 * rr + b) for rr in range(10)], axis=0)
-            for a in range(2)
-            for b in range(2)
-        ],
-        axis=1,
-    ).astype(BF)
+def conv1_rows(x4_ref, w1_ref, fn_ref, first, rows):
+    for pp, n, taps in PAIRS:
+        out = conv1(
+            lambda h, s, b: x4_ref[
+                pp + h : pp + h + n, s, first + b : first + b + rows
+            ].reshape(n * rows * 64, 256),
+            w1_ref,
+            taps,
+        )
+        for q in range(2):
+            fn_ref[pp : pp + n, q] = out[:, q * 128 : (q + 1) * 128].reshape(n, rows, 64, 128)
+
+
+def reduce1(taps, wr1_ref):
+    lhs = jnp.concatenate(taps, axis=1).astype(BF)
     return leaky(mm(lhs, wr1_ref[...])).astype(BF)
-
-
-def put_planes(out, pp, rows, fn_ref):
-    for q in range(2):
-        fn_ref[2 * pp + q] = out[:, q * 128 : (q + 1) * 128].reshape(rows, 64, 128)
 
 
 def own_kernel(
@@ -195,14 +194,12 @@
     window_columns(dt_ref, lhs_ref, 8)
 
     def store(g, row, lanes, values):
-        x4_ref[g, row, :, lanes] = values
+        x4_ref[g // 2, g % 2, row, :, lanes] = values
         if row in (0, 1, 6, 7):
             x4b_ref[g, row if row < 2 else row - 4, :, lanes] = values
 
     lift(lhs_ref, wl_ref, 8, 64, BF, store)
-    for pp in range(4):
-        out = conv1(lambda plane, b: x4_ref[plane, b : b + 6].reshape(384, 256), w1_ref, pp)
-        put_planes(out, pp, 6, fn_ref)
+    conv1_rows(x4_ref, w1_ref, fn_ref, 0, 6)
 
 
 def top_kernel(up_ref, x4b_ref, wl_ref, w1_ref, fn_ref, lup_ref, rup_ref, dt_ref, lhs_ref, x4_ref):
@@ -210,16 +207,12 @@
     window_columns(dt_ref, lhs_ref, 8)
 
     def store(g, row, lanes, values):
-        x4_ref[g, row, :, lanes] = values
+        x4_ref[g // 2, g % 2, row, :, lanes] = values
 
     lift(lhs_ref, wl_ref, 8, 64, BF, store)
     for plane in range(8):
-        x4_ref[plane, 8:10] = x4b_ref[plane, 0:2]
-    for pp in range(4):
-        out = conv1(
-            lambda plane, b: x4_ref[plane, 1 + b : 8 + b].reshape(448, 256), w1_ref, pp
-        )
-        put_planes(out, pp, 7, fn_ref)
+        x4_ref[plane // 2, plane % 2, 8:10] = x4b_ref[plane, 0:2]
+    conv1_rows(x4_ref, w1_ref, fn_ref, 1, 7)
 
 
 def bottom_kernel(
@@ -228,31 +221,44 @@
     window_columns(dt_ref, lhs_ref, 8)
 
     def store(g, row, lanes, values):
-        x4_ref[g, row + 2, :, lanes] = values
+        x4_ref[g // 2, g % 2, row + 2, :, lanes] = values
 
     lift(lhs_ref, wl_ref, 8, 64, BF, store)
     for plane in range(8):
-        x4_ref[plane, 0:2] = x4b_ref[plane, 2:4]
-    for pp in range(4):
-        out = conv1(lambda plane, b: x4_ref[plane, b : b + 7].reshape(448, 256), w1_ref, pp)
-        put_planes(out, pp, 7, fn_ref)
+        x4_ref[plane // 2, plane % 2, 0:2] = x4b_ref[plane, 2:4]
+    conv1_rows(x4_ref, w1_ref, fn_ref, 0, 7)
     for pp in range(4):
 
         def row_of(a, row):
             if row < 7:
-                return fnt_ref[2 * pp + a, row]
+                return fnt_ref[pp, a, row]
             if row < 13:
-                return fno_ref[2 * pp + a, row - 7]
-            return fn_ref[2 * pp + a, row - 13]
-
-        mid_ref[pp] = reduce1(row_of, wr1_ref).reshape(10, 64, 128)
+                return fno_ref[pp, a, row - 7]
+            return fn_ref[pp, a, row - 13]
+
+        taps = [
+            jnp.concatenate([row_of(a, 2 * rr + b) for rr in range(10)], axis=0)
+            for a in range(2)
+            for b in range(2)
+        ]
+        mid_ref[pp] = reduce1(taps, wr1_ref).reshape(10, 64, 128)
 
 
 def outer_kernel(
-    lrecv_ref, left_ref, right_ref, rrecv_ref, wl_ref, w1_ref, wr1_ref, main_ref, w2_ref, wr2_ref, w3_ref,
-    fn_ref, skip_ref, chunk_ref,
-    de_ref, dw_ref, lhs_ref, x4_ref, me_ref, mf_ref, xm_ref, ms_ref, cf_ref,
+    lrecv_ref, left_ref, right_ref, rrecv_ref, wl_ref, w1_ref, wr1_ref, main_ref, wr2_ref, w3_ref, c2_hbm,
+    edge_ref, skip_ref, chunk_ref,
+    de_ref, dw_ref, lhs_ref, x4_ref, fn_ref, me_ref, mf_ref, xm_ref, ms_ref, cf_ref, w2_ref, sem,
 ):
+    copies = [
+        pltpu.make_async_copy(
+            c2_hbm, w2_ref.at[3 * q : 3 * q + 9, :, q * 128 : (q + 1) * 128], sem.at[q]
+        )
+        for q in range(2)
+    ]
+    for copy in copies:
+        copy.start()
+    w2_ref[0:3, :, 128:256] = jnp.zeros((3, 384, 128), BF)
+    w2_ref[9:12, :, 0:128] = jnp.zeros((3, 384, 128), BF)
     de_ref[:, 0:8] = lrecv_ref[...]
     de_ref[:, 8:16] = left_ref[...]
     de_ref[:, 16:24] = right_ref[...]
@@ -272,29 +278,37 @@
                 axis=1,
             ).astype(BF)
 
+    zero = jnp.zeros((24, 8, 256), F32)
+    x4_ref[0, 1] = zero
+    x4_ref[5, 0] = zero
+
     def store(g, row, lanes, values):
-        x4_ref[g % 8, g // 8 * 8 + row, :, lanes] = values
+        x4_ref[1 + g % 8 // 2, g % 2, g // 8 * 8 + row, :, lanes] = values
 
     lift(lhs_ref, wl_ref, 24, 8, F32, store)
-    for pp in range(4):
-        out = conv1(
-            lambda plane, b: x4_ref[plane, 1 + b : 21 + b].reshape(160, 256), w1_ref, pp
-        ).astype(F32)
-        for q in range(2):
-            fn_ref[2 * pp + q] = out[:, q * 128 : (q + 1) * 128].reshape(20, 8, 128)
-        mid = reduce1(lambda a, row: fn_ref[2 * pp + a, row], wr1_ref)
-        me_ref[pp] = mid.astype(F32).reshape(10, 8, 128)
+    out = conv1(
+        lambda h, s, b: x4_ref[1 + h : 5 + h, s, 1 + b : 21 + b].reshape(640, 256),
+        w1_ref,
+        range(4),
+    ).astype(F32)
+    for q in range(2):
+        fn_ref[:, q] = out[:, q * 128 : (q + 1) * 128].reshape(4, 10, 2, 8, 128)
+    edge_ref[...] = fn_ref[:, :, 3:7].reshape(8, 8, 8, 128)
+    taps = [fn_ref[:, a, :, b].reshape(320, 128) for a in range(2) for b in range(2)]
+    me_ref[...] = reduce1(taps, wr1_ref).astype(F32).reshape(4, 10, 8, 128)
 
     def merge(n, carry):
         plane, row = n // 10, n % 10
-        mf_ref[n, 3:67] = main_ref[plane, row].astype(F32)
-        mf_ref[n, 0:4] = me_ref[plane, row, 0:4]
-        mf_ref[n, 66:70] = me_ref[plane, row, 4:8]
+        mf_ref[n, 16:80] = main_ref[plane, row].astype(F32)
+        mf_ref[n, 13:17] = me_ref[plane, row, 0:4]
+        mf_ref[n, 79:83] = me_ref[plane, row, 4:8]
         for c in range(3):
-            xm_ref[plane, row, :, c * 128 : (c + 1) * 128] = mf_ref[n, c : c + 80].astype(BF)
+            xm_ref[plane, row, :, c * 128 : (c + 1) * 128] = mf_ref[n, 7 + c : 87 + c].astype(BF)
         return carry
 
     lax.fori_loop(0, 40, merge, 0)
+    for copy in copies:
+        copy.wait()
     for half in range(2):
         taps = range(1, 4) if half == 0 else range(0, 3)
         lhs = jnp.concatenate(
@@ -308,10 +322,9 @@
         weight = w2_ref[taps[0] * 3 : taps[0] * 3 + 9].reshape(3456, 256)
         out = rounded(leaky(mm(lhs, weight)))
         for q in range(2):
-            ms_ref[2 * half + q] = out[:, q * 128 : (q + 1) * 128].reshape(8, 80, 128)
+            ms_ref[2 * half + q, :, 0:80] = out[:, q * 128 : (q + 1) * 128].reshape(8, 80, 128)
     for plane in range(4):
-        for row in range(4):
-            skip_ref[plane, row] = ms_ref[plane, row + 2, 2:66].astype(BF)
+        skip_ref[plane] = ms_ref[plane, 2:6, 8:72].astype(BF)
     taps = []
     for a in range(2):
         for b in range(2):
@@ -319,7 +332,7 @@
                 taps.append(
                     jnp.concatenate(
                         [
-                            ms_ref[2 * plane + a, 2 * row + b, pl.ds(c, 40, stride=2)]
+                            ms_ref[2 * plane + a, 2 * row + b, pl.ds(6 + c, 40, stride=2)]
                             for plane in range(2)
                             for row in range(4)
                         ],
@@ -358,8 +371,8 @@
         now = []
         for r in (row, row + 1):
             v = (fnt_ref[0, 0] if r == 0 else fnb_ref[0, 0] if r == 7 else fno_ref[0, r - 1]).astype(F32)
-            v = jnp.where(pair == 0, edge_ref[0, r + 6, 3:4], v)
-            now.append(jnp.where(pair == 63, edge_ref[0, r + 6, 4:5], v))
+            v = jnp.where(pair == 0, edge_ref[0, r, 3:4], v)
+            now.append(jnp.where(pair == 63, edge_ref[0, r, 4:5], v))
         wide_ref[row // 2, pl.ds(0, 64, stride=2), :] = jnp.where(
             lane < 64, now[0], pltpu.roll(now[1], 64, 1)
         )
@@ -394,14 +407,14 @@
     own = disp.reshape(24, 8, 128)
     up = shift(own, "wide", 1)
     strip = struct((8, 8, 128), F32)
-    fine_scratch = (VMEM((2, 512, 256), BF), VMEM((8, 10, 64, 256), BF))
+    fine_scratch = (VMEM((2, 512, 256), BF), VMEM((4, 2, 10, 64, 256), BF))
     turn_scratch = (VMEM((8, 144, 128), F32),)
     stay = lambda x: pltpu.with_memory_space_constraint(x, pltpu.HBM)
     x4b, fno, lown, rown, wl, w1 = call(
         own_kernel,
         (
             struct((8, 4, 64, 256), BF),
-            struct((8, 6, 64, 128), BF),
+            struct((4, 2, 6, 64, 128), BF),
             strip,
             strip,
             struct((4, 256, 256), BF),
@@ -424,18 +437,9 @@
     )
     again, x4b = lax.optimization_barrier((own, x4b))
     down = shift(again, "wide", -1)
-    w2 = call(
-        middle_weights_kernel,
-        struct((12, 384, 256), BF),
-        (conv2_w.reshape(9, 384, 128),),
-        6,
-        name="middle_weights",
-        flops=10**6,
-        nbytes=4 * 10**6,
-    )
     fnt, lup, rup = call(
         top_kernel,
-        (struct((8, 7, 64, 128), BF), strip, strip),
+        (struct((4, 2, 7, 64, 128), BF), strip, strip),
         (up, x4b, wl, w1),
         12,
         scratch=turn_scratch + fine_scratch,
@@ -457,7 +461,7 @@
     wr1 = reduce1_w.reshape(512, 128)
     fnb, mid = call(
         bottom_kernel,
-        (struct((8, 7, 64, 128), BF), struct((4, 10, 64, 128), BF)),
+        (struct((4, 2, 7, 64, 128), BF), struct((4, 10, 64, 128), BF)),
         (dt, x4b, fnt, fno, wl, w1, wr1),
         14,
         scratch=fine_scratch,
@@ -467,22 +471,27 @@
     )
     edge, skip, chunk = call(
         outer_kernel,
-        (struct((8, 20, 8, 128), F32), struct((4, 4, 64, 128), BF), struct((64, 4, 128), BF)),
+        (struct((8, 8, 8, 128), F32), struct((4, 4, 64, 128), BF), struct((64, 4, 128), BF)),
         (
-            lrecv, left, right, rrecv, wl, w1, wr1, mid, w2,
+            lrecv, left, right, rrecv, wl, w1, wr1, mid,
             reduce2_w.reshape(1024, 256), conv3_w.reshape(3, 2304, 256),
+            stay(conv2_w.reshape(9, 384, 128)),
         ),
-        24,
+        26,
+        last=pltpu.HBM,
         scratch=(
             VMEM((24, 32, 128), F32),
             VMEM((2, 24, 16, 128), F32),
             VMEM((2, 192, 256), BF),
-            VMEM((8, 24, 8, 256), F32),
+            VMEM((6, 2, 24, 8, 256), F32),
+            VMEM((4, 2, 10, 2, 8, 128), F32),
             VMEM((4, 10, 8, 128), F32),
-            VMEM((40, 88, 128), F32),
+            VMEM((40, 96, 128), F32),
             VMEM((4, 10, 80, 384), BF),
-            VMEM((4, 8, 80, 128), F32),
+            VMEM((4, 8, 88, 128), F32),
             VMEM((2, 4, 40, 256), F32),
+            VMEM((12, 384, 256), BF),
+            pltpu.SemaphoreType.DMA((2,)),
         ),
         name="middle_and_coarse",
         flops=6 * 10**9,
@@ -497,14 +506,19 @@
             pl.BlockSpec((1, 1, 64, 128), lambda p: (p, 6, 0, 0)),
             pl.BlockSpec((1, 6, 64, 128), lambda p: (p, 0, 0, 0)),
             pl.BlockSpec((1, 1, 64, 128), lambda p: (p, 0, 0, 0)),
-            pl.BlockSpec((1, 20, 8, 128), lambda p: (p, 0, 0, 0)),
+            pl.BlockSpec((1, 8, 8, 128), lambda p: (p, 0, 0, 0)),
         ],
         out_specs=pl.BlockSpec((64, 1, 8, 128), lambda p: (0, p, 0, 0)),
         scratch_shapes=[VMEM((4, 128, 128), F32), VMEM((64, 8, 128), F32)],
         compiler_params=pltpu.CompilerParams(vmem_limit_bytes=6 * MIB),
         cost_estimate=pl.CostEstimate(flops=10**8, bytes_accessed=3 * 10**6, transcendentals=0),
         name="finest_layout",
-    )(fnt, fno, fnb, edge)
+    )(
+        fnt.reshape(8, 7, 64, 128),
+        fno.reshape(8, 6, 64, 128),
+        fnb.reshape(8, 7, 64, 128),
+        edge,
+    )
     coarse = call(
         coarse_kernel,
         struct((4, 2, 32, 128), BF),

time: 54.5 us -> 54.1 us (level)
  Pallas kernels: 26.5 us -> 25.8 us
    pallas_call x7 -> x6, Pallas kernels: 22.2 us -> 21.5 us  [call(): pl.pallas_call(kernel, out_shape=outs, in_specs=[pl.BlockSpec(memory_spac...]
where the time goes in v3:
time: 54.1 us; the launch traced here: 53.9 us
  Pallas kernels  25.8 us (48%)
  starting transfers between devices  20.2 us (37%)
  waiting for transfers between devices  7.11 us (13%)
  between operations  0.72 us (1%)
    pallas_call x6, Pallas kernels, call(): pl.pallas_call(kernel, out_shape=outs, in_specs=[pl.BlockSpec(memory_spac...  21.5 us
    ppermute x4, starting transfers between devices, shift(): lax.ppermute(array, axis, [(i, (i + step) % peers) for i in range(peers)])  13.3 us
    all_to_all x1, starting transfers between devices, on_device(): received = lax.all_to_all(chunk, 'wide', 0, 0, tiled=True)  6.93 us
    all_to_all x1, waiting for transfers between devices, on_device(): received = lax.all_to_all(chunk, 'wide', 0, 0, tiled=True)  5.47 us
    pallas_call x1, Pallas kernels, on_device(): pl.pallas_call(finest_kernel, grid=(8,), out_shape=struct((64, 8, 8, 128)...  4.31 us
    ppermute x4, waiting for transfers between devices, shift(): lax.ppermute(array, axis, [(i, (i + step) % peers) for i in range(peers)])  1.64 us
  transfers between devices with their start and end apart: 5, of which 2 were waited for; matrix products, arithmetic and copies ran while one was open for 0% of the time, Pallas kernels for 30%

profile of v3, /device:TPU:1, one launch (start us, length us, event | category | flops | bytes accessed | tf_op | source)
XLA Modules:
  0.0 53.9 jit_solution(7485585089311455962)
XLA Ops:
  0.6 2.5 %collective-permute-start = (f32[24,8,128]{2,1,0:T(8,128)}, f32[24,8,128]{2,1,0:T(8,128)S(1)}, u32[]{:S(2)}, u32[]{:S(2)}) collective-permute-start(f32[24,8,128]{2,1,0:T(8,128)} %bitcast.21), channel_id=1, source_target_pairs={{0,4},{4,8},{8,12},{12,16},{16,20},{20,24},{24,28},{28,32},{32,36}... | collective-permute-start | bytes 294920 | tf_op jit(solution)/shard_map/ppermute | solution.py:399
  3.2 0.0 copy-start.3
  3.2 4.6 %fine_own_rows.1 = (bf16[8,4,64,256]{3,2,1,0:T(8,128)(2,1)S(1)}, bf16[4,2,6,64,128]{4,3,2,1,0:T(8,128)(2,1)S(1)}, f32[8,8,128]{2,1,0:T(8,128)S(1)}, f32[8,8,128]...) custom-call(f32[24,8,128]{2,1,0:T(8,128)} %bitcast.22, f32[3,64]{1,0:T(4,128)} %lift_hbm.1, ...), custom_call_target="tpu_custom_call" | custom-call | flops 2000000000 | bytes 6000000 | tf_op jit(solution)/shard_map/fine_own_rows/pallas_call | solution.py:28
  7.8 0.0 copy-done.3
  7.8 7.4 %collective-permute-start.1 = (f32[24,8,128]{2,1,0:T(8,128)S(1)}, f32[24,8,128]{2,1,0:T(8,128)S(1)}, u32[]{:S(2)}, u32[]{:S(2)}) collective-permute-start(f32[24,8,128]{2,1,0:T(8,128)S(1)} %bitcast.23), channel_id=1, source_target_pairs={{0,252},{4,0},{8,4},{12,8},{16,12},{20,16},{24,20},{28,24},{32,28}... | collective-permute-start | bytes 294920 | tf_op jit(solution)/shard_map/ppermute | solution.py:399
  15.2 0.0 collective-permute-done.up_ref
  15.2 0.0 copy-start.2
  15.2 3.3 %fine_top_rows.1 = (bf16[4,2,7,64,128]{4,3,2,1,0:T(8,128)(2,1)S(1)}, f32[8,8,128]{2,1,0:T(8,128)S(1)}, f32[8,8,128]{2,1,0:T(8,128)S(1)}) custom-call(f32[24,8,128]{2,1,0:T(8,128)S(1)} %collective-permute-done.up_ref, bf16[8,4,64,256]{3,2,1,0:T(8,128)(2,1)S(1)} %get-tuple-element.23.x4b_ref, bf16[4,256,256]{2,1,0:T(8,128)(2,1)S(1)} %get-tuple-element.24.wl_ref, ...), custom_call_target="tpu_custom_call" | custom-call | flops 3000000000 | bytes 6000000 | tf_op jit(solution)/shard_map/fine_top_rows/pallas_call | solution.py:28
  18.5 0.0 collective-permute-done.1.down_ref
  18.5 0.2 columns_to_rows.1
  18.7 3.4 %collective-permute-start.2 = (f32[24,8,128]{2,1,0:T(8,128)S(1)}, f32[24,8,128]{2,1,0:T(8,128)S(1)}, u32[]{:S(2)}, u32[]{:S(2)}) collective-permute-start(f32[24,8,128]{2,1,0:T(8,128)S(1)} %get-tuple-element.35.right_ref), channel_id=1, source_target_pairs={{0,1},{1,2},{2,3},{3,0},{4,5},{5,6},{6,7},{7,4},{8,9},{9,10},{10,1... | collective-permute-start | bytes 294920 | tf_op jit(solution)/shard_map/ppermute | solution.py:399
  22.1 0.0 collective-permute-start.3
  22.1 0.0 copy-done.2
  22.1 0.0 copy-start.1
  22.1 3.9 %fine_bottom_rows.1 = (bf16[4,2,7,64,128]{4,3,2,1,0:T(8,128)(2,1)S(1)}, bf16[4,10,64,128]{3,2,1,0:T(8,128)(2,1)S(1)}) custom-call(f32[8,144,128]{2,1,0:T(8,128)S(1)} %get-tuple-element.33.dt_ref, bf16[8,4,64,256]{3,2,1,0:T(8,128)(2,1)S(1)} %get-tuple-element.23.x4b_ref, bf16[4,2,7,64,128]{4,3,2,1,0:T(8,128)(2,1)S(1)} %get-tuple-element.26.fnt_ref, ...), custom_call_target="tpu_custom_call" | custom-call | flops 8000000000 | bytes 6000000 | tf_op jit(solution)/shard_map/fine_bottom_rows/pallas_call | solution.py:28
  26.0 0.0 collective-permute-done.2.lrecv_ref
  26.0 1.6 %collective-permute-done.3.rrecv_ref = f32[24,8,128]{2,1,0:T(8,128)S(1)} collective-permute-done((f32[24,8,128]{2,1,0:T(8,128)S(1)}, f32[24,8,128]{2,1,0:T(8,128)S(1)}, u32[]{:S(2)}, u32[]{:S(2)}) %collective-permute-start.3) | collective-permute-done | bytes 98336 | tf_op jit(solution)/shard_map/ppermute | solution.py:399
  27.6 0.0 copy-done
  27.7 0.0 copy-done.1
  27.7 8.6 %middle_and_coarse.1 = (f32[8,8,8,128]{3,2,1,0:T(8,128)S(1)}, bf16[4,4,64,128]{3,2,1,0:T(8,128)(2,1)}, bf16[64,4,128]{2,1,0:T(4,128)(2,1)}) custom-call(f32[24,8,128]{2,1,0:T(8,128)S(1)} %collective-permute-done.2.lrecv_ref, f32[24,8,128]{2,1,0:T(8,128)S(1)} %get-tuple-element.36.left_ref, f32[24,8,128]{2,1,0:T(8,128)S(1)} %get-tuple-element.35.right_ref, ...), custom_call_target="tpu_custom_call" | custom-call | flops 6000000000 | bytes 12000000 | tf_op jit(solution)/shard_map/middle_and_coarse/pallas_call | solution.py:28
  36.3 6.9 %all-to-all-start = ((bf16[64,4,128]{2,1,0:T(4,128)(2,1)}), bf16[64,4,128]{2,1,0:T(4,128)(2,1)S(1)}, u32[]{:S(2)}, u32[]{:S(2)}) async-start(bf16[64,4,128]{2,1,0:T(4,128)(2,1)} %get-tuple-element.40), calls=%async_computation | async-start | bytes 131072 | tf_op jit(solution)/shard_map/all_to_all | solution.py:500
  43.2 4.3 %finest_layout.1 = bf16[64,8,8,128]{3,2,1,0:T(8,128)(2,1)} custom-call(bf16[8,7,64,128]{3,2,1,0:T(8,128)(2,1)S(1)} %bitcast.11, bf16[8,6,64,128]{3,2,1,0:T(8,128)(2,1)S(1)} %bitcast.13, bf16[8,7,64,128]{3,2,1,0:T(8,128)(2,1)S(1)} %bitcast.12, f32[8,8,8,128]{3,2,1,0:T(8,128)S(1)} %get-tuple-element.38.edge_ref), custom_call_target="tpu_custom_call" | custom-call | flops 100000000 | bytes 3000000 | tf_op jit(solution)/shard_map/finest_layout/pallas_call | solution.py:501
  47.5 5.5 %all-to-all-done.in_ref = bf16[64,4,128]{2,1,0:T(4,128)(2,1)S(1)} async-done(((bf16[64,4,128]{2,1,0:T(4,128)(2,1)}), bf16[64,4,128]{2,1,0:T(4,128)(2,1)S(1)}, u32[]{:S(2)}, u32[]{:S(2)}) %all-to-all-start) | async-done | bytes 65568 | tf_op jit(solution)/shard_map/all_to_all | solution.py:500
  53.0 0.9 %coarse_layout.1 = bf16[4,2,32,128]{3,2,1,0:T(8,128)(2,1)} custom-call(bf16[64,4,128]{2,1,0:T(4,128)(2,1)S(1)} %all-to-all-done.in_ref), custom_call_target="tpu_custom_call" | custom-call | flops 1000000 | bytes 200000 | tf_op jit(solution)/shard_map/coarse_layout/pallas_call | solution.py:28
  (1 shorter events, 0.0 us)
Async XLA Ops:
  0.6 14.6 %collective-permute-start = (f32[24,8,128]{2,1,0:T(8,128)}, f32[24,8,128]{2,1,0:T(8,128)S(1)}, u32[]{:S(2)}, u32[]{:S(2)}) collective-permute-start(f32[24,8,128]{2,1,0:T(8,128)} %bitcast.21), channel_id=1, source_target_pairs={{0,4},{4,8},{8,12},{12,16},{16,20},{20,24},{24,28},{28,32},{32,36}... | collective-permute-start | bytes 294920 | tf_op jit(solution)/shard_map/ppermute | solution.py:399
  3.2 4.6 %copy-start.3 = (f32[3,8,8,128]{3,2,1,0:T(8,128)S(1)}, f32[3,8,8,128]{3,2,1,0:T(8,128)}, u32[]{:S(2)}) copy-start(f32[3,8,8,128]{3,2,1,0:T(8,128)} %param.7) | copy-start | bytes 294916
  7.8 10.7 %collective-permute-start.1 = (f32[24,8,128]{2,1,0:T(8,128)S(1)}, f32[24,8,128]{2,1,0:T(8,128)S(1)}, u32[]{:S(2)}, u32[]{:S(2)}) collective-permute-start(f32[24,8,128]{2,1,0:T(8,128)S(1)} %bitcast.23), channel_id=1, source_target_pairs={{0,252},{4,0},{8,4},{12,8},{16,12},{20,16},{24,20},{28,24},{32,28}... | collective-permute-start | bytes 294920 | tf_op jit(solution)/shard_map/ppermute | solution.py:399
  15.2 6.9 %copy-start.2 = (bf16[2,2,2,64,128]{4,3,2,1,0:T(8,128)(2,1)S(1)}, bf16[2,2,2,64,128]{4,3,2,1,0:T(8,128)(2,1)}, u32[]{:S(2)}) copy-start(bf16[2,2,2,64,128]{4,3,2,1,0:T(8,128)(2,1)} %param.10) | copy-start | bytes 393220
  18.7 7.3 %collective-permute-start.2 = (f32[24,8,128]{2,1,0:T(8,128)S(1)}, f32[24,8,128]{2,1,0:T(8,128)S(1)}, u32[]{:S(2)}, u32[]{:S(2)}) collective-permute-start(f32[24,8,128]{2,1,0:T(8,128)S(1)} %get-tuple-element.35.right_ref), channel_id=1, source_target_pairs={{0,1},{1,2},{2,3},{3,0},{4,5},{5,6},{6,7},{7,4},{8,9},{9,10},{10,1... | collective-permute-start | bytes 294920 | tf_op jit(solution)/shard_map/ppermute | solution.py:399
  22.1 5.5 %collective-permute-start.3 = (f32[24,8,128]{2,1,0:T(8,128)S(1)}, f32[24,8,128]{2,1,0:T(8,128)S(1)}, u32[]{:S(2)}, u32[]{:S(2)}) collective-permute-start(f32[24,8,128]{2,1,0:T(8,128)S(1)} %get-tuple-element.36.left_ref), channel_id=1, source_target_pairs={{0,3},{1,0},{2,1},{3,2},{4,7},{5,4},{6,5},{7,6},{8,11},{9,8},{10,9... | collective-permute-start | bytes 294920 | tf_op jit(solution)/shard_map/ppermute | solution.py:399
  22.1 5.5 %copy-start = (bf16[3,3,3,256,256]{4,3,2,1,0:T(8,128)(2,1)S(1)}, bf16[3,3,3,256,256]{4,3,2,1,0:T(8,128)(2,1)}, u32[]{:S(2)}) copy-start(bf16[3,3,3,256,256]{4,3,2,1,0:T(8,128)(2,1)} %param.13) | copy-start | bytes 10616836
  22.1 5.5 %copy-start.1 = (bf16[2,2,2,128,256]{4,3,2,1,0:T(8,128)(2,1)S(1)}, bf16[2,2,2,128,256]{4,3,2,1,0:T(8,128)(2,1)}, u32[]{:S(2)}) copy-start(bf16[2,2,2,128,256]{4,3,2,1,0:T(8,128)(2,1)} %param.12) | copy-start | bytes 1572868
  36.3 16.7 %all-to-all-start = ((bf16[64,4,128]{2,1,0:T(4,128)(2,1)}), bf16[64,4,128]{2,1,0:T(4,128)(2,1)S(1)}, u32[]{:S(2)}, u32[]{:S(2)}) async-start(bf16[64,4,128]{2,1,0:T(4,128)(2,1)} %get-tuple-element.40), calls=%async_computation | async-start | bytes 131072 | tf_op jit(solution)/shard_map/all_to_all | solution.py:500

commit v4 on v3

--- a/solution.py
+++ b/solution.py
@@ -297,16 +297,13 @@
     taps = [fn_ref[:, a, :, b].reshape(320, 128) for a in range(2) for b in range(2)]
     me_ref[...] = reduce1(taps, wr1_ref).astype(F32).reshape(4, 10, 8, 128)
 
-    def merge(n, carry):
+    for n in range(40):
         plane, row = n // 10, n % 10
         mf_ref[n, 16:80] = main_ref[plane, row].astype(F32)
         mf_ref[n, 13:17] = me_ref[plane, row, 0:4]
         mf_ref[n, 79:83] = me_ref[plane, row, 4:8]
         for c in range(3):
             xm_ref[plane, row, :, c * 128 : (c + 1) * 128] = mf_ref[n, 7 + c : 87 + c].astype(BF)
-        return carry
-
-    lax.fori_loop(0, 40, merge, 0)
     for copy in copies:
         copy.wait()
     for half in range(2):
@@ -389,9 +386,10 @@
     all_in = in_ref[...].astype(F32)
     for c in range(4):
         v = all_in[:, c, :]
-        y_ref[pl.ds(0, 64, stride=2), :] = v
-        y_ref[pl.ds(1, 64, stride=2), :] = pltpu.roll(v, 64, 1)
-        out_ref[c] = y_ref[...].T[0:64].reshape(2, 32, 128).astype(BF)
+        y_ref[c, pl.ds(0, 64, stride=2), :] = v
+        y_ref[c, pl.ds(1, 64, stride=2), :] = pltpu.roll(v, 64, 1)
+    for c in range(4):
+        out_ref[c] = y_ref[c].T[0:64].reshape(2, 32, 128).astype(BF)
 
 
 def shift(array, axis, step):
@@ -524,7 +522,7 @@
         struct((4, 2, 32, 128), BF),
         (received,),
         4,
-        scratch=(VMEM((128, 128), F32),),
+        scratch=(VMEM((4, 128, 128), F32),),
         name="coarse_layout",
         flops=10**6,
         nbytes=2 * 10**5,

time: 54.1 us -> 53.7 us (level)
  no operation moved by 1% of the time
where the time goes in v4:
time: 53.7 us; the launch traced here: 53.5 us
  Pallas kernels  25.4 us (47%)
  starting transfers between devices  20.2 us (38%)
  waiting for transfers between devices  7.11 us (13%)
  between operations  0.72 us (1%)
    pallas_call x6, Pallas kernels, call(): pl.pallas_call(kernel, out_shape=outs, in_specs=[pl.BlockSpec(memory_spac...  21.1 us
    ppermute x4, starting transfers between devices, shift(): lax.ppermute(array, axis, [(i, (i + step) % peers) for i in range(peers)])  13.3 us
    all_to_all x1, starting transfers between devices, on_device(): received = lax.all_to_all(chunk, 'wide', 0, 0, tiled=True)  6.93 us
    all_to_all x1, waiting for transfers between devices, on_device(): received = lax.all_to_all(chunk, 'wide', 0, 0, tiled=True)  5.47 us
    pallas_call x1, Pallas kernels, on_device(): pl.pallas_call(finest_kernel, grid=(8,), out_shape=struct((64, 8, 8, 128)...  4.31 us
    ppermute x4, waiting for transfers between devices, shift(): lax.ppermute(array, axis, [(i, (i + step) % peers) for i in range(peers)])  1.64 us
  transfers between devices with their start and end apart: 5, of which 2 were waited for; matrix products, arithmetic and copies ran while one was open for 0% of the time, Pallas kernels for 30%

profile of v4, /device:TPU:1, one launch (start us, length us, event | category | flops | bytes accessed | tf_op | source)
XLA Modules:
  0.0 53.5 jit_solution(4053005530342339801)
XLA Ops:
  0.6 2.5 %collective-permute-start = (f32[24,8,128]{2,1,0:T(8,128)}, f32[24,8,128]{2,1,0:T(8,128)S(1)}, u32[]{:S(2)}, u32[]{:S(2)}) collective-permute-start(f32[24,8,128]{2,1,0:T(8,128)} %bitcast.21), channel_id=1, source_target_pairs={{0,4},{4,8},{8,12},{12,16},{16,20},{20,24},{24,28},{28,32},{32,36}... | collective-permute-start | bytes 294920 | tf_op jit(solution)/shard_map/ppermute | solution.py:397
  3.2 0.0 copy-start.3
  3.2 4.6 %fine_own_rows.1 = (bf16[8,4,64,256]{3,2,1,0:T(8,128)(2,1)S(1)}, bf16[4,2,6,64,128]{4,3,2,1,0:T(8,128)(2,1)S(1)}, f32[8,8,128]{2,1,0:T(8,128)S(1)}, f32[8,8,128]...) custom-call(f32[24,8,128]{2,1,0:T(8,128)} %bitcast.22, f32[3,64]{1,0:T(4,128)} %lift_hbm.1, ...), custom_call_target="tpu_custom_call" | custom-call | flops 2000000000 | bytes 6000000 | tf_op jit(solution)/shard_map/fine_own_rows/pallas_call | solution.py:28
  7.8 0.0 copy-done.3
  7.8 7.4 %collective-permute-start.1 = (f32[24,8,128]{2,1,0:T(8,128)S(1)}, f32[24,8,128]{2,1,0:T(8,128)S(1)}, u32[]{:S(2)}, u32[]{:S(2)}) collective-permute-start(f32[24,8,128]{2,1,0:T(8,128)S(1)} %bitcast.23), channel_id=1, source_target_pairs={{0,252},{4,0},{8,4},{12,8},{16,12},{20,16},{24,20},{28,24},{32,28}... | collective-permute-start | bytes 294920 | tf_op jit(solution)/shard_map/ppermute | solution.py:397
  15.2 0.0 collective-permute-done.up_ref
  15.2 0.0 copy-start.2
  15.2 3.3 %fine_top_rows.1 = (bf16[4,2,7,64,128]{4,3,2,1,0:T(8,128)(2,1)S(1)}, f32[8,8,128]{2,1,0:T(8,128)S(1)}, f32[8,8,128]{2,1,0:T(8,128)S(1)}) custom-call(f32[24,8,128]{2,1,0:T(8,128)S(1)} %collective-permute-done.up_ref, bf16[8,4,64,256]{3,2,1,0:T(8,128)(2,1)S(1)} %get-tuple-element.23.x4b_ref, bf16[4,256,256]{2,1,0:T(8,128)(2,1)S(1)} %get-tuple-element.24.wl_ref, ...), custom_call_target="tpu_custom_call" | custom-call | flops 3000000000 | bytes 6000000 | tf_op jit(solution)/shard_map/fine_top_rows/pallas_call | solution.py:28
  18.5 0.0 collective-permute-done.1.down_ref
  18.5 0.2 columns_to_rows.1
  18.7 3.4 %collective-permute-start.2 = (f32[24,8,128]{2,1,0:T(8,128)S(1)}, f32[24,8,128]{2,1,0:T(8,128)S(1)}, u32[]{:S(2)}, u32[]{:S(2)}) collective-permute-start(f32[24,8,128]{2,1,0:T(8,128)S(1)} %get-tuple-element.35.right_ref), channel_id=1, source_target_pairs={{0,1},{1,2},{2,3},{3,0},{4,5},{5,6},{6,7},{7,4},{8,9},{9,10},{10,1... | collective-permute-start | bytes 294920 | tf_op jit(solution)/shard_map/ppermute | solution.py:397
  22.1 0.0 collective-permute-start.3
  22.1 0.0 copy-done.2
  22.1 0.0 copy-start.1
  22.1 3.9 %fine_bottom_rows.1 = (bf16[4,2,7,64,128]{4,3,2,1,0:T(8,128)(2,1)S(1)}, bf16[4,10,64,128]{3,2,1,0:T(8,128)(2,1)S(1)}) custom-call(f32[8,144,128]{2,1,0:T(8,128)S(1)} %get-tuple-element.33.dt_ref, bf16[8,4,64,256]{3,2,1,0:T(8,128)(2,1)S(1)} %get-tuple-element.23.x4b_ref, bf16[4,2,7,64,128]{4,3,2,1,0:T(8,128)(2,1)S(1)} %get-tuple-element.26.fnt_ref, ...), custom_call_target="tpu_custom_call" | custom-call | flops 8000000000 | bytes 6000000 | tf_op jit(solution)/shard_map/fine_bottom_rows/pallas_call | solution.py:28
  26.0 0.0 collective-permute-done.2.lrecv_ref
  26.0 1.6 %collective-permute-done.3.rrecv_ref = f32[24,8,128]{2,1,0:T(8,128)S(1)} collective-permute-done((f32[24,8,128]{2,1,0:T(8,128)S(1)}, f32[24,8,128]{2,1,0:T(8,128)S(1)}, u32[]{:S(2)}, u32[]{:S(2)}) %collective-permute-start.3) | collective-permute-done | bytes 98336 | tf_op jit(solution)/shard_map/ppermute | solution.py:397
  27.6 0.0 copy-done
  27.7 0.0 copy-done.1
  27.7 8.2 %middle_and_coarse.1 = (f32[8,8,8,128]{3,2,1,0:T(8,128)S(1)}, bf16[4,4,64,128]{3,2,1,0:T(8,128)(2,1)}, bf16[64,4,128]{2,1,0:T(4,128)(2,1)}) custom-call(f32[24,8,128]{2,1,0:T(8,128)S(1)} %collective-permute-done.2.lrecv_ref, f32[24,8,128]{2,1,0:T(8,128)S(1)} %get-tuple-element.36.left_ref, f32[24,8,128]{2,1,0:T(8,128)S(1)} %get-tuple-element.35.right_ref, ...), custom_call_target="tpu_custom_call" | custom-call | flops 6000000000 | bytes 12000000 | tf_op jit(solution)/shard_map/middle_and_coarse/pallas_call | solution.py:28
  35.9 6.9 %all-to-all-start = ((bf16[64,4,128]{2,1,0:T(4,128)(2,1)}), bf16[64,4,128]{2,1,0:T(4,128)(2,1)S(1)}, u32[]{:S(2)}, u32[]{:S(2)}) async-start(bf16[64,4,128]{2,1,0:T(4,128)(2,1)} %get-tuple-element.40), calls=%async_computation | async-start | bytes 131072 | tf_op jit(solution)/shard_map/all_to_all | solution.py:498
  42.8 4.3 %finest_layout.1 = bf16[64,8,8,128]{3,2,1,0:T(8,128)(2,1)} custom-call(bf16[8,7,64,128]{3,2,1,0:T(8,128)(2,1)S(1)} %bitcast.11, bf16[8,6,64,128]{3,2,1,0:T(8,128)(2,1)S(1)} %bitcast.13, bf16[8,7,64,128]{3,2,1,0:T(8,128)(2,1)S(1)} %bitcast.12, f32[8,8,8,128]{3,2,1,0:T(8,128)S(1)} %get-tuple-element.38.edge_ref), custom_call_target="tpu_custom_call" | custom-call | flops 100000000 | bytes 3000000 | tf_op jit(solution)/shard_map/finest_layout/pallas_call | solution.py:499
  47.1 5.5 %all-to-all-done.in_ref = bf16[64,4,128]{2,1,0:T(4,128)(2,1)S(1)} async-done(((bf16[64,4,128]{2,1,0:T(4,128)(2,1)}), bf16[64,4,128]{2,1,0:T(4,128)(2,1)S(1)}, u32[]{:S(2)}, u32[]{:S(2)}) %all-to-all-start) | async-done | bytes 65568 | tf_op jit(solution)/shard_map/all_to_all | solution.py:498
  52.6 0.9 %coarse_layout.1 = bf16[4,2,32,128]{3,2,1,0:T(8,128)(2,1)} custom-call(bf16[64,4,128]{2,1,0:T(4,128)(2,1)S(1)} %all-to-all-done.in_ref), custom_call_target="tpu_custom_call" | custom-call | flops 1000000 | bytes 200000 | tf_op jit(solution)/shard_map/coarse_layout/pallas_call | solution.py:28
  (1 shorter events, 0.0 us)
Async XLA Ops:
  0.6 14.6 %collective-permute-start = (f32[24,8,128]{2,1,0:T(8,128)}, f32[24,8,128]{2,1,0:T(8,128)S(1)}, u32[]{:S(2)}, u32[]{:S(2)}) collective-permute-start(f32[24,8,128]{2,1,0:T(8,128)} %bitcast.21), channel_id=1, source_target_pairs={{0,4},{4,8},{8,12},{12,16},{16,20},{20,24},{24,28},{28,32},{32,36}... | collective-permute-start | bytes 294920 | tf_op jit(solution)/shard_map/ppermute | solution.py:397
  3.2 4.6 %copy-start.3 = (f32[3,8,8,128]{3,2,1,0:T(8,128)S(1)}, f32[3,8,8,128]{3,2,1,0:T(8,128)}, u32[]{:S(2)}) copy-start(f32[3,8,8,128]{3,2,1,0:T(8,128)} %param.7) | copy-start | bytes 294916
  7.8 10.7 %collective-permute-start.1 = (f32[24,8,128]{2,1,0:T(8,128)S(1)}, f32[24,8,128]{2,1,0:T(8,128)S(1)}, u32[]{:S(2)}, u32[]{:S(2)}) collective-permute-start(f32[24,8,128]{2,1,0:T(8,128)S(1)} %bitcast.23), channel_id=1, source_target_pairs={{0,252},{4,0},{8,4},{12,8},{16,12},{20,16},{24,20},{28,24},{32,28}... | collective-permute-start | bytes 294920 | tf_op jit(solution)/shard_map/ppermute | solution.py:397
  15.2 6.9 %copy-start.2 = (bf16[2,2,2,64,128]{4,3,2,1,0:T(8,128)(2,1)S(1)}, bf16[2,2,2,64,128]{4,3,2,1,0:T(8,128)(2,1)}, u32[]{:S(2)}) copy-start(bf16[2,2,2,64,128]{4,3,2,1,0:T(8,128)(2,1)} %param.10) | copy-start | bytes 393220
  18.7 7.3 %collective-permute-start.2 = (f32[24,8,128]{2,1,0:T(8,128)S(1)}, f32[24,8,128]{2,1,0:T(8,128)S(1)}, u32[]{:S(2)}, u32[]{:S(2)}) collective-permute-start(f32[24,8,128]{2,1,0:T(8,128)S(1)} %get-tuple-element.35.right_ref), channel_id=1, source_target_pairs={{0,1},{1,2},{2,3},{3,0},{4,5},{5,6},{6,7},{7,4},{8,9},{9,10},{10,1... | collective-permute-start | bytes 294920 | tf_op jit(solution)/shard_map/ppermute | solution.py:397
  22.1 5.5 %collective-permute-start.3 = (f32[24,8,128]{2,1,0:T(8,128)S(1)}, f32[24,8,128]{2,1,0:T(8,128)S(1)}, u32[]{:S(2)}, u32[]{:S(2)}) collective-permute-start(f32[24,8,128]{2,1,0:T(8,128)S(1)} %get-tuple-element.36.left_ref), channel_id=1, source_target_pairs={{0,3},{1,0},{2,1},{3,2},{4,7},{5,4},{6,5},{7,6},{8,11},{9,8},{10,9... | collective-permute-start | bytes 294920 | tf_op jit(solution)/shard_map/ppermute | solution.py:397
  22.1 5.5 %copy-start = (bf16[3,3,3,256,256]{4,3,2,1,0:T(8,128)(2,1)S(1)}, bf16[3,3,3,256,256]{4,3,2,1,0:T(8,128)(2,1)}, u32[]{:S(2)}) copy-start(bf16[3,3,3,256,256]{4,3,2,1,0:T(8,128)(2,1)} %param.13) | copy-start | bytes 10616836
  22.1 5.5 %copy-start.1 = (bf16[2,2,2,128,256]{4,3,2,1,0:T(8,128)(2,1)S(1)}, bf16[2,2,2,128,256]{4,3,2,1,0:T(8,128)(2,1)}, u32[]{:S(2)}) copy-start(bf16[2,2,2,128,256]{4,3,2,1,0:T(8,128)(2,1)} %param.12) | copy-start | bytes 1572868
  35.9 16.7 %all-to-all-start = ((bf16[64,4,128]{2,1,0:T(4,128)(2,1)}), bf16[64,4,128]{2,1,0:T(4,128)(2,1)S(1)}, u32[]{:S(2)}, u32[]{:S(2)}) async-start(bf16[64,4,128]{2,1,0:T(4,128)(2,1)} %get-tuple-element.40), calls=%async_computation | async-start | bytes 131072 | tf_op jit(solution)/shard_map/all_to_all | solution.py:498

commit v5 on v4

--- a/solution.py
+++ b/solution.py
@@ -174,8 +174,8 @@
 
 
 def own_kernel(
-    own_hbm, lift_hbm, c1_hbm, x4b_ref, fn_ref, lown_ref, rown_ref, wl_ref, w1_ref,
-    dt_ref, lhs_ref, x4_ref, own_ref, lift_ref, c1_ref, sems,
+    own_hbm, lift_hbm, c1_hbm, x4_ref, lown_ref, rown_ref, wl_ref, w1_ref,
+    dt_ref, lhs_ref, own_ref, lift_ref, c1_ref, sems,
 ):
     copies = [
         pltpu.make_async_copy(src, dst, sems.at[n])
@@ -195,10 +195,11 @@
 
     def store(g, row, lanes, values):
         x4_ref[g // 2, g % 2, row, :, lanes] = values
-        if row in (0, 1, 6, 7):
-            x4b_ref[g, row if row < 2 else row - 4, :, lanes] = values
 
     lift(lhs_ref, wl_ref, 8, 64, BF, store)
+
+
+def own_rows_kernel(x4_ref, w1_ref, fn_ref):
     conv1_rows(x4_ref, w1_ref, fn_ref, 0, 6)
 
 
@@ -211,7 +212,7 @@
 
     lift(lhs_ref, wl_ref, 8, 64, BF, store)
     for plane in range(8):
-        x4_ref[plane // 2, plane % 2, 8:10] = x4b_ref[plane, 0:2]
+        x4_ref[plane // 2, plane % 2, 8:10] = x4b_ref[plane // 2, plane % 2, 0:2]
     conv1_rows(x4_ref, w1_ref, fn_ref, 1, 7)
 
 
@@ -225,7 +226,7 @@
 
     lift(lhs_ref, wl_ref, 8, 64, BF, store)
     for plane in range(8):
-        x4_ref[plane // 2, plane % 2, 0:2] = x4b_ref[plane, 2:4]
+        x4_ref[plane // 2, plane % 2, 0:2] = x4b_ref[plane // 2, plane % 2, 6:8]
     conv1_rows(x4_ref, w1_ref, fn_ref, 0, 7)
     for pp in range(4):
 
@@ -408,11 +409,10 @@
     fine_scratch = (VMEM((2, 512, 256), BF), VMEM((4, 2, 10, 64, 256), BF))
     turn_scratch = (VMEM((8, 144, 128), F32),)
     stay = lambda x: pltpu.with_memory_space_constraint(x, pltpu.HBM)
-    x4b, fno, lown, rown, wl, w1 = call(
+    x4b, lown, rown, wl, w1 = call(
         own_kernel,
         (
-            struct((8, 4, 64, 256), BF),
-            struct((4, 2, 6, 64, 128), BF),
+            struct((4, 2, 8, 64, 256), BF),
             strip,
             strip,
             struct((4, 256, 256), BF),
@@ -421,14 +421,14 @@
         (stay(own), stay(lift_w), stay(conv1_w.reshape(9, 192, 64))),
         14,
         scratch=turn_scratch
-        + fine_scratch
         + (
+            VMEM((2, 512, 256), BF),
             VMEM((24, 8, 128), F32),
             VMEM((3, 64), F32),
             VMEM((9, 192, 64), BF),
             pltpu.SemaphoreType.DMA((3,)),
         ),
-        name="fine_own_rows",
+        name="fine_own_lift",
         flops=2 * 10**9,
         nbytes=6 * 10**6,
         space=pltpu.HBM,
@@ -455,7 +455,18 @@
         nbytes=2 * 10**6,
     )
     rrecv = shift(left, "narrow", -1)
-    lrecv = shift(right, "narrow", 1)
+    fno = call(
+        own_rows_kernel,
+        struct((4, 2, 6, 64, 128), BF),
+        (x4b, w1),
+        8,
+        name="fine_own_rows",
+        flops=2 * 10**9,
+        nbytes=6 * 10**6,
+    )
+    again, fno = lax.optimization_barrier((right, fno))
+    lrecv = shift(again, "narrow", 1)
+    dt, rrecv = lax.optimization_barrier((dt, rrecv))
     wr1 = reduce1_w.reshape(512, 128)
     fnb, mid = call(
         bottom_kernel,

time: 53.7 us -> 52.1 us (0.970)
  waiting for transfers between devices: 7.11 us -> 5.4 us
    ppermute x4, waiting for transfers between devices: 1.64 us -> 0.23 us  [shift(): lax.ppermute(array, axis, [(i, (i + step) % peers) for i in range(peers)])]
    ppermute x4, starting transfers between devices: 13.3 us -> 13.9 us  [shift(): lax.ppermute(array, axis, [(i, (i + step) % peers) for i in range(peers)])]
    pallas_call x6 -> x7, Pallas kernels: 21.1 us -> 21.2 us  [call(): pl.pallas_call(kernel, out_shape=outs, in_specs=[pl.BlockSpec(memory_spac...]
  transfers between devices with their start and end apart: 5 -> 5, of which waited for: 2 -> 2; matrix products, arithmetic and copies ran while one was open for 0% -> 0% of each run, Pallas kernels for 30% -> 31%
where the time goes in v5:
time: 52.1 us; the launch traced here: 51.9 us
  Pallas kernels  25.5 us (49%)
  starting transfers between devices  20.3 us (39%)
  waiting for transfers between devices  5.4 us (10%)
  between operations  0.74 us (1%)
    pallas_call x7, Pallas kernels, call(): pl.pallas_call(kernel, out_shape=outs, in_specs=[pl.BlockSpec(memory_spac...  21.2 us
    ppermute x4, starting transfers between devices, shift(): lax.ppermute(array, axis, [(i, (i + step) % peers) for i in range(peers)])  13.9 us
    all_to_all x1, starting transfers between devices, on_device(): received = lax.all_to_all(chunk, 'wide', 0, 0, tiled=True)  6.44 us
    all_to_all x1, waiting for transfers between devices, on_device(): received = lax.all_to_all(chunk, 'wide', 0, 0, tiled=True)  5.17 us
    pallas_call x1, Pallas kernels, on_device(): pl.pallas_call(finest_kernel, grid=(8,), out_shape=struct((64, 8, 8, 128)...  4.31 us
  transfers between devices with their start and end apart: 5, of which 2 were waited for; matrix products, arithmetic and copies ran while one was open for 0% of the time, Pallas kernels for 31%

profile of v5, /device:TPU:1, one launch (start us, length us, event | category | flops | bytes accessed | tf_op | source)
XLA Modules:
  0.0 51.9 jit_solution(12929790790225353998)
XLA Ops:
  0.6 2.5 %collective-permute-start = (f32[24,8,128]{2,1,0:T(8,128)}, f32[24,8,128]{2,1,0:T(8,128)S(1)}, u32[]{:S(2)}, u32[]{:S(2)}) collective-permute-start(f32[24,8,128]{2,1,0:T(8,128)} %bitcast.21), channel_id=1, source_target_pairs={{0,4},{4,8},{8,12},{12,16},{16,20},{20,24},{24,28},{28,32},{32,36}... | collective-permute-start | bytes 294920 | tf_op jit(solution)/shard_map/ppermute | solution.py:398
  3.2 0.0 copy-start.3
  3.2 2.4 %fine_own_lift.1 = (bf16[4,2,8,64,256]{4,3,2,1,0:T(8,128)(2,1)S(1)}, f32[8,8,128]{2,1,0:T(8,128)S(1)}, f32[8,8,128]{2,1,0:T(8,128)S(1)}, bf16[4,256,256]{2,1,0:T(8,128)(2,1)S(1)}, bf16[12,256,256]{2,1,0:T(8,128)(2,1)S(1)}) custom-call(f32[24,8,128]{2,1,0:T(8,128)} %bitcast.22, f32[3,64]{1,0:T(4,128)} %lift_hbm.1, bf16[9,192,64]{2,1,0:T(8,128)(2,1)} %bitcast.20), custom_call_target="tpu_custom_call" | custom-call | flops 2000000000 | bytes 6000000 | tf_op jit(solution)/shard_map/fine_own_lift/pallas_call | solution.py:28
  5.6 0.0 copy-done.3
  5.6 7.4 %collective-permute-start.1 = (f32[24,8,128]{2,1,0:T(8,128)S(1)}, f32[24,8,128]{2,1,0:T(8,128)S(1)}, u32[]{:S(2)}, u32[]{:S(2)}) collective-permute-start(f32[24,8,128]{2,1,0:T(8,128)S(1)} %bitcast.23), channel_id=1, source_target_pairs={{0,252},{4,0},{8,4},{12,8},{16,12},{20,16},{24,20},{28,24},{32,28}... | collective-permute-start | bytes 294920 | tf_op jit(solution)/shard_map/ppermute | solution.py:398
  13.0 0.2 collective-permute-done.up_ref
  13.2 3.3 %fine_top_rows.1 = (bf16[4,2,7,64,128]{4,3,2,1,0:T(8,128)(2,1)S(1)}, f32[8,8,128]{2,1,0:T(8,128)S(1)}, f32[8,8,128]{2,1,0:T(8,128)S(1)}) custom-call(f32[24,8,128]{2,1,0:T(8,128)S(1)} %collective-permute-done.up_ref, bf16[4,2,8,64,256]{4,3,2,1,0:T(8,128)(2,1)S(1)} %get-tuple-element.26.x4b_ref.x4_ref, bf16[4,256,256]{2,1,0:T(8,128)(2,1)S(1)} %get-tuple-element.27.wl_ref, ...), custom_call_target="tpu_custom_call" | custom-call | flops 3000000000 | bytes 6000000 | tf_op jit(solution)/shard_map/fine_top_rows/pallas_call | solution.py:28
  16.5 0.0 collective-permute-done.1.down_ref
  16.5 0.2 columns_to_rows.1
  16.7 0.0 copy-start.2
  16.7 1.3 %collective-permute-start.2 = (f32[24,8,128]{2,1,0:T(8,128)S(1)}, f32[24,8,128]{2,1,0:T(8,128)S(1)}, u32[]{:S(2)}, u32[]{:S(2)}) collective-permute-start(f32[24,8,128]{2,1,0:T(8,128)S(1)} %get-tuple-element.38.left_ref), channel_id=1, source_target_pairs={{0,3},{1,0},{2,1},{3,2},{4,7},{5,4},{6,5},{7,6},{8,11},{9,8},{10,9... | collective-permute-start | bytes 294920 | tf_op jit(solution)/shard_map/ppermute | solution.py:398
  18.1 2.3 %fine_own_rows.1.fno_ref = bf16[4,2,6,64,128]{4,3,2,1,0:T(8,128)(2,1)S(1)} custom-call(bf16[4,2,8,64,256]{4,3,2,1,0:T(8,128)(2,1)S(1)} %get-tuple-element.26.x4b_ref.x4_ref, bf16[12,256,256]{2,1,0:T(8,128)(2,1)S(1)} %get-tuple-element.28.w1_ref), custom_call_target="tpu_custom_call" | custom-call | flops 2000000000 | bytes 6000000 | tf_op jit(solution)/shard_map/fine_own_rows/pallas_call | solution.py:28
  20.4 2.6 %collective-permute-start.3 = (f32[24,8,128]{2,1,0:T(8,128)S(1)}, f32[24,8,128]{2,1,0:T(8,128)S(1)}, u32[]{:S(2)}, u32[]{:S(2)}) collective-permute-start(f32[24,8,128]{2,1,0:T(8,128)S(1)} %get-tuple-element.41.right_ref), channel_id=1, source_target_pairs={{0,1},{1,2},{2,3},{3,0},{4,5},{5,6},{6,7},{7,4},{8,9},{9,10},{10,1... | collective-permute-start | bytes 294920 | tf_op jit(solution)/shard_map/ppermute | solution.py:398
  23.0 0.0 collective-permute-done.2.rrecv_ref
  23.0 0.0 copy-done.2
  23.0 3.9 %fine_bottom_rows.1 = (bf16[4,2,7,64,128]{4,3,2,1,0:T(8,128)(2,1)S(1)}, bf16[4,10,64,128]{3,2,1,0:T(8,128)(2,1)S(1)}) custom-call(f32[8,144,128]{2,1,0:T(8,128)S(1)} %get-tuple-element.39.dt_ref, bf16[4,2,8,64,256]{4,3,2,1,0:T(8,128)(2,1)S(1)} %get-tuple-element.26.x4b_ref.x4_ref, bf16[4,2,7,64,128]{4,3,2,1,0:T(8,128)(2,1)S(1)} %get-tuple-element.29.fnt_ref, ...), custom_call_target="tpu_custom_call" | custom-call | flops 8000000000 | bytes 6000000 | tf_op jit(solution)/shard_map/fine_bottom_rows/pallas_call | solution.py:28
  26.9 0.0 collective-permute-done.3.lrecv_ref
  26.9 0.0 copy-done
  26.9 0.0 copy-done.1
  26.9 8.2 %middle_and_coarse.1 = (f32[8,8,8,128]{3,2,1,0:T(8,128)S(1)}, bf16[4,4,64,128]{3,2,1,0:T(8,128)(2,1)}, bf16[64,4,128]{2,1,0:T(4,128)(2,1)}) custom-call(f32[24,8,128]{2,1,0:T(8,128)S(1)} %collective-permute-done.3.lrecv_ref, f32[24,8,128]{2,1,0:T(8,128)S(1)} %get-tuple-element.38.left_ref, f32[24,8,128]{2,1,0:T(8,128)S(1)} %get-tuple-element.41.right_ref, ...), custom_call_target="tpu_custom_call" | custom-call | flops 6000000000 | bytes 12000000 | tf_op jit(solution)/shard_map/middle_and_coarse/pallas_call | solution.py:28
  35.1 6.4 %all-to-all-start = ((bf16[64,4,128]{2,1,0:T(4,128)(2,1)}), bf16[64,4,128]{2,1,0:T(4,128)(2,1)S(1)}, u32[]{:S(2)}, u32[]{:S(2)}) async-start(bf16[64,4,128]{2,1,0:T(4,128)(2,1)} %get-tuple-element.46), calls=%async_computation | async-start | bytes 131072 | tf_op jit(solution)/shard_map/all_to_all | solution.py:509
  41.5 4.3 %finest_layout.1 = bf16[64,8,8,128]{3,2,1,0:T(8,128)(2,1)} custom-call(bf16[8,7,64,128]{3,2,1,0:T(8,128)(2,1)S(1)} %bitcast.11, bf16[8,6,64,128]{3,2,1,0:T(8,128)(2,1)S(1)} %bitcast.13, bf16[8,7,64,128]{3,2,1,0:T(8,128)(2,1)S(1)} %bitcast.12, f32[8,8,8,128]{3,2,1,0:T(8,128)S(1)} %get-tuple-element.44.edge_ref), custom_call_target="tpu_custom_call" | custom-call | flops 100000000 | bytes 3000000 | tf_op jit(solution)/shard_map/finest_layout/pallas_call | solution.py:510
  45.9 5.2 %all-to-all-done.in_ref = bf16[64,4,128]{2,1,0:T(4,128)(2,1)S(1)} async-done(((bf16[64,4,128]{2,1,0:T(4,128)(2,1)}), bf16[64,4,128]{2,1,0:T(4,128)(2,1)S(1)}, u32[]{:S(2)}, u32[]{:S(2)}) %all-to-all-start) | async-done | bytes 65568 | tf_op jit(solution)/shard_map/all_to_all | solution.py:509
  51.0 0.9 %coarse_layout.1 = bf16[4,2,32,128]{3,2,1,0:T(8,128)(2,1)} custom-call(bf16[64,4,128]{2,1,0:T(4,128)(2,1)S(1)} %all-to-all-done.in_ref), custom_call_target="tpu_custom_call" | custom-call | flops 1000000 | bytes 200000 | tf_op jit(solution)/shard_map/coarse_layout/pallas_call | solution.py:28
  (2 shorter events, 0.0 us)
Async XLA Ops:
  0.6 12.6 %collective-permute-start = (f32[24,8,128]{2,1,0:T(8,128)}, f32[24,8,128]{2,1,0:T(8,128)S(1)}, u32[]{:S(2)}, u32[]{:S(2)}) collective-permute-start(f32[24,8,128]{2,1,0:T(8,128)} %bitcast.21), channel_id=1, source_target_pairs={{0,4},{4,8},{8,12},{12,16},{16,20},{20,24},{24,28},{28,32},{32,36}... | collective-permute-start | bytes 294920 | tf_op jit(solution)/shard_map/ppermute | solution.py:398
  3.2 2.4 %copy-start.3 = (f32[3,8,8,128]{3,2,1,0:T(8,128)S(1)}, f32[3,8,8,128]{3,2,1,0:T(8,128)}, u32[]{:S(2)}) copy-start(f32[3,8,8,128]{3,2,1,0:T(8,128)} %param.7) | copy-start | bytes 294916
  5.6 10.9 %collective-permute-start.1 = (f32[24,8,128]{2,1,0:T(8,128)S(1)}, f32[24,8,128]{2,1,0:T(8,128)S(1)}, u32[]{:S(2)}, u32[]{:S(2)}) collective-permute-start(f32[24,8,128]{2,1,0:T(8,128)S(1)} %bitcast.23), channel_id=1, source_target_pairs={{0,252},{4,0},{8,4},{12,8},{16,12},{20,16},{24,20},{28,24},{32,28}... | collective-permute-start | bytes 294920 | tf_op jit(solution)/shard_map/ppermute | solution.py:398
  16.7 6.2 %copy-start.2 = (bf16[2,2,2,64,128]{4,3,2,1,0:T(8,128)(2,1)S(1)}, bf16[2,2,2,64,128]{4,3,2,1,0:T(8,128)(2,1)}, u32[]{:S(2)}) copy-start(bf16[2,2,2,64,128]{4,3,2,1,0:T(8,128)(2,1)} %param.10) | copy-start | bytes 393220
  16.7 6.2 %collective-permute-start.2 = (f32[24,8,128]{2,1,0:T(8,128)S(1)}, f32[24,8,128]{2,1,0:T(8,128)S(1)}, u32[]{:S(2)}, u32[]{:S(2)}) collective-permute-start(f32[24,8,128]{2,1,0:T(8,128)S(1)} %get-tuple-element.38.left_ref), channel_id=1, source_target_pairs={{0,3},{1,0},{2,1},{3,2},{4,7},{5,4},{6,5},{7,6},{8,11},{9,8},{10,9... | collective-permute-start | bytes 294920 | tf_op jit(solution)/shard_map/ppermute | solution.py:398
  20.4 6.5 %collective-permute-start.3 = (f32[24,8,128]{2,1,0:T(8,128)S(1)}, f32[24,8,128]{2,1,0:T(8,128)S(1)}, u32[]{:S(2)}, u32[]{:S(2)}) collective-permute-start(f32[24,8,128]{2,1,0:T(8,128)S(1)} %get-tuple-element.41.right_ref), channel_id=1, source_target_pairs={{0,1},{1,2},{2,3},{3,0},{4,5},{5,6},{6,7},{7,4},{8,9},{9,10},{10,1... | collective-permute-start | bytes 294920 | tf_op jit(solution)/shard_map/ppermute | solution.py:398
  23.0 3.9 %copy-start = (bf16[3,3,3,256,256]{4,3,2,1,0:T(8,128)(2,1)S(1)}, bf16[3,3,3,256,256]{4,3,2,1,0:T(8,128)(2,1)}, u32[]{:S(2)}) copy-start(bf16[3,3,3,256,256]{4,3,2,1,0:T(8,128)(2,1)} %param.13) | copy-start | bytes 10616836
  23.0 3.9 %copy-start.1 = (bf16[2,2,2,128,256]{4,3,2,1,0:T(8,128)(2,1)S(1)}, bf16[2,2,2,128,256]{4,3,2,1,0:T(8,128)(2,1)}, u32[]{:S(2)}) copy-start(bf16[2,2,2,128,256]{4,3,2,1,0:T(8,128)(2,1)} %param.12) | copy-start | bytes 1572868
  35.1 15.9 %all-to-all-start = ((bf16[64,4,128]{2,1,0:T(4,128)(2,1)}), bf16[64,4,128]{2,1,0:T(4,128)(2,1)S(1)}, u32[]{:S(2)}, u32[]{:S(2)}) async-start(bf16[64,4,128]{2,1,0:T(4,128)(2,1)} %get-tuple-element.46), calls=%async_computation | async-start | bytes 131072 | tf_op jit(solution)/shard_map/all_to_all | solution.py:509

commit v6 on v5

--- a/solution.py
+++ b/solution.py
@@ -102,18 +102,18 @@
     for plane in range(8):
         out = turned(src, plane)
         dt_ref[plane, 8:136] = out
-        left_ref[plane] = out[0:8]
-        right_ref[plane] = out[120:128]
+        left_ref[plane] = out[0:8].astype(left_ref.dtype)
+        right_ref[plane] = out[120:128].astype(right_ref.dtype)
     dt_ref[:, 0:8, :] = jnp.zeros((8, 8, 128), F32)
     dt_ref[:, 136:144, :] = jnp.zeros((8, 8, 128), F32)
 
 
 def turn_kernel(down_ref, lup_ref, rup_ref, lown_ref, rown_ref, dt_ref, left_ref, right_ref):
     turn_block(down_ref, dt_ref, left_ref.at[16:24], right_ref.at[16:24])
-    left_ref[0:8] = lup_ref[...]
-    right_ref[0:8] = rup_ref[...]
-    left_ref[8:16] = lown_ref[...]
-    right_ref[8:16] = rown_ref[...]
+    left_ref[0:8] = lup_ref[...].astype(BF)
+    right_ref[0:8] = rup_ref[...].astype(BF)
+    left_ref[8:16] = lown_ref[...].astype(BF)
+    right_ref[8:16] = rown_ref[...].astype(BF)
 
 
 def window_columns(dt_ref, lhs_ref, groups):
@@ -260,10 +260,10 @@
         copy.start()
     w2_ref[0:3, :, 128:256] = jnp.zeros((3, 384, 128), BF)
     w2_ref[9:12, :, 0:128] = jnp.zeros((3, 384, 128), BF)
-    de_ref[:, 0:8] = lrecv_ref[...]
-    de_ref[:, 8:16] = left_ref[...]
-    de_ref[:, 16:24] = right_ref[...]
-    de_ref[:, 24:32] = rrecv_ref[...]
+    de_ref[:, 0:8] = lrecv_ref[...].astype(F32)
+    de_ref[:, 8:16] = left_ref[...].astype(F32)
+    de_ref[:, 16:24] = right_ref[...].astype(F32)
+    de_ref[:, 24:32] = rrecv_ref[...].astype(F32)
     for half in range(2):
         dw_ref[half, :, 0:8] = de_ref[:, 1 + 2 * half : 9 + 2 * half]
         dw_ref[half, :, 8:16] = de_ref[:, 21 + 2 * half : 29 + 2 * half]
@@ -447,7 +447,7 @@
     )
     dt, left, right = call(
         turn_kernel,
-        (struct((8, 144, 128), F32), struct((24, 8, 128), F32), struct((24, 8, 128), F32)),
+        (struct((8, 144, 128), F32), struct((24, 8, 128), BF), struct((24, 8, 128), BF)),
         (down, lup, rup, lown, rown),
         6,
         name="columns_to_rows",

time: 52.1 us -> 52.4 us (level)
  no operation moved by 1% of the time
where the time goes in v6:
time: 52.4 us; the launch traced here: 52.2 us
  Pallas kernels  25.5 us (49%)
  starting transfers between devices  20.3 us (39%)
  waiting for transfers between devices  5.7 us (11%)
  between operations  0.74 us (1%)
    pallas_call x7, Pallas kernels, call(): pl.pallas_call(kernel, out_shape=outs, in_specs=[pl.BlockSpec(memory_spac...  21.2 us
    ppermute x4, starting transfers between devices, shift(): lax.ppermute(array, axis, [(i, (i + step) % peers) for i in range(peers)])  13.9 us
    all_to_all x1, starting transfers between devices, on_device(): received = lax.all_to_all(chunk, 'wide', 0, 0, tiled=True)  6.43 us
    all_to_all x1, waiting for transfers between devices, on_device(): received = lax.all_to_all(chunk, 'wide', 0, 0, tiled=True)  5.47 us
    pallas_call x1, Pallas kernels, on_device(): pl.pallas_call(finest_kernel, grid=(8,), out_shape=struct((64, 8, 8, 128)...  4.31 us
  transfers between devices with their start and end apart: 5, of which 2 were waited for; matrix products, arithmetic and copies ran while one was open for 0% of the time, Pallas kernels for 31%

profile of v6, /device:TPU:1, one launch (start us, length us, event | category | flops | bytes accessed | tf_op | source)
XLA Modules:
  0.0 52.2 jit_solution(5428498770482030002)
XLA Ops:
  0.6 2.5 %collective-permute-start = (f32[24,8,128]{2,1,0:T(8,128)}, f32[24,8,128]{2,1,0:T(8,128)S(1)}, u32[]{:S(2)}, u32[]{:S(2)}) collective-permute-start(f32[24,8,128]{2,1,0:T(8,128)} %bitcast.21), channel_id=1, source_target_pairs={{0,4},{4,8},{8,12},{12,16},{16,20},{20,24},{24,28},{28,32},{32,36}... | collective-permute-start | bytes 294920 | tf_op jit(solution)/shard_map/ppermute | solution.py:398
  3.2 0.0 copy-start.3
  3.2 2.4 %fine_own_lift.1 = (bf16[4,2,8,64,256]{4,3,2,1,0:T(8,128)(2,1)S(1)}, f32[8,8,128]{2,1,0:T(8,128)S(1)}, f32[8,8,128]{2,1,0:T(8,128)S(1)}, bf16[4,256,256]{2,1,0:T(8,128)(2,1)S(1)}, bf16[12,256,256]{2,1,0:T(8,128)(2,1)S(1)}) custom-call(f32[24,8,128]{2,1,0:T(8,128)} %bitcast.22, f32[3,64]{1,0:T(4,128)} %lift_hbm.1, bf16[9,192,64]{2,1,0:T(8,128)(2,1)} %bitcast.20), custom_call_target="tpu_custom_call" | custom-call | flops 2000000000 | bytes 6000000 | tf_op jit(solution)/shard_map/fine_own_lift/pallas_call | solution.py:28
  5.6 0.0 copy-done.3
  5.6 7.4 %collective-permute-start.1 = (f32[24,8,128]{2,1,0:T(8,128)S(1)}, f32[24,8,128]{2,1,0:T(8,128)S(1)}, u32[]{:S(2)}, u32[]{:S(2)}) collective-permute-start(f32[24,8,128]{2,1,0:T(8,128)S(1)} %bitcast.23), channel_id=1, source_target_pairs={{0,252},{4,0},{8,4},{12,8},{16,12},{20,16},{24,20},{28,24},{32,28}... | collective-permute-start | bytes 294920 | tf_op jit(solution)/shard_map/ppermute | solution.py:398
  13.0 0.2 collective-permute-done.up_ref
  13.2 3.3 %fine_top_rows.1 = (bf16[4,2,7,64,128]{4,3,2,1,0:T(8,128)(2,1)S(1)}, f32[8,8,128]{2,1,0:T(8,128)S(1)}, f32[8,8,128]{2,1,0:T(8,128)S(1)}) custom-call(f32[24,8,128]{2,1,0:T(8,128)S(1)} %collective-permute-done.up_ref, bf16[4,2,8,64,256]{4,3,2,1,0:T(8,128)(2,1)S(1)} %get-tuple-element.26.x4b_ref.x4_ref, bf16[4,256,256]{2,1,0:T(8,128)(2,1)S(1)} %get-tuple-element.27.wl_ref, ...), custom_call_target="tpu_custom_call" | custom-call | flops 3000000000 | bytes 6000000 | tf_op jit(solution)/shard_map/fine_top_rows/pallas_call | solution.py:28
  16.5 0.0 collective-permute-done.1.down_ref
  16.5 0.2 columns_to_rows.1
  16.7 0.0 copy-start.2
  16.7 1.3 %collective-permute-start.2 = (bf16[24,8,128]{2,1,0:T(8,128)(2,1)S(1)}, bf16[24,8,128]{2,1,0:T(8,128)(2,1)S(1)}, u32[]{:S(2)}, u32[]{:S(2)}) collective-permute-start(bf16[24,8,128]{2,1,0:T(8,128)(2,1)S(1)} %get-tuple-element.38.left_ref), channel_id=1, source_target_pairs={{0,3},{1,0},{2,1},{3,2},{4,7},{5,4},{6,5},{7,6},{8,11},{9,8},{10,9... | collective-permute-start | bytes 147464 | tf_op jit(solution)/shard_map/ppermute | solution.py:398
  18.1 2.3 %fine_own_rows.1.fno_ref = bf16[4,2,6,64,128]{4,3,2,1,0:T(8,128)(2,1)S(1)} custom-call(bf16[4,2,8,64,256]{4,3,2,1,0:T(8,128)(2,1)S(1)} %get-tuple-element.26.x4b_ref.x4_ref, bf16[12,256,256]{2,1,0:T(8,128)(2,1)S(1)} %get-tuple-element.28.w1_ref), custom_call_target="tpu_custom_call" | custom-call | flops 2000000000 | bytes 6000000 | tf_op jit(solution)/shard_map/fine_own_rows/pallas_call | solution.py:28
  20.4 2.6 %collective-permute-start.3 = (bf16[24,8,128]{2,1,0:T(8,128)(2,1)S(1)}, bf16[24,8,128]{2,1,0:T(8,128)(2,1)S(1)}, u32[]{:S(2)}, u32[]{:S(2)}) collective-permute-start(bf16[24,8,128]{2,1,0:T(8,128)(2,1)S(1)} %get-tuple-element.41.right_ref), channel_id=1, source_target_pairs={{0,1},{1,2},{2,3},{3,0},{4,5},{5,6},{6,7},{7,4},{8,9},{9,10},{10,1... | collective-permute-start | bytes 147464 | tf_op jit(solution)/shard_map/ppermute | solution.py:398
  23.0 0.0 collective-permute-done.2.rrecv_ref
  23.0 0.0 copy-done.2
  23.0 3.9 %fine_bottom_rows.1 = (bf16[4,2,7,64,128]{4,3,2,1,0:T(8,128)(2,1)S(1)}, bf16[4,10,64,128]{3,2,1,0:T(8,128)(2,1)S(1)}) custom-call(f32[8,144,128]{2,1,0:T(8,128)S(1)} %get-tuple-element.39.dt_ref, bf16[4,2,8,64,256]{4,3,2,1,0:T(8,128)(2,1)S(1)} %get-tuple-element.26.x4b_ref.x4_ref, bf16[4,2,7,64,128]{4,3,2,1,0:T(8,128)(2,1)S(1)} %get-tuple-element.29.fnt_ref, ...), custom_call_target="tpu_custom_call" | custom-call | flops 8000000000 | bytes 6000000 | tf_op jit(solution)/shard_map/fine_bottom_rows/pallas_call | solution.py:28
  26.9 0.0 collective-permute-done.3.lrecv_ref
  26.9 0.0 copy-done
  26.9 0.0 copy-done.1
  26.9 8.2 %middle_and_coarse.1 = (f32[8,8,8,128]{3,2,1,0:T(8,128)S(1)}, bf16[4,4,64,128]{3,2,1,0:T(8,128)(2,1)}, bf16[64,4,128]{2,1,0:T(4,128)(2,1)}) custom-call(bf16[24,8,128]{2,1,0:T(8,128)(2,1)S(1)} %collective-permute-done.3.lrecv_ref, bf16[24,8,128]{2,1,0:T(8,128)(2,1)S(1)} %get-tuple-element.38.left_ref, bf16[24,8,128]{2,1,0:T(8,128)(2,1)S(1)} %get-tuple-element.41.right_ref, ...), custom_call_target="tpu_custom_call" | custom-call | flops 6000000000 | bytes 12000000 | tf_op jit(solution)/shard_map/middle_and_coarse/pallas_call | solution.py:28
  35.1 6.4 %all-to-all-start = ((bf16[64,4,128]{2,1,0:T(4,128)(2,1)}), bf16[64,4,128]{2,1,0:T(4,128)(2,1)S(1)}, u32[]{:S(2)}, u32[]{:S(2)}) async-start(bf16[64,4,128]{2,1,0:T(4,128)(2,1)} %get-tuple-element.46), calls=%async_computation | async-start | bytes 131072 | tf_op jit(solution)/shard_map/all_to_all | solution.py:509
  41.5 4.3 %finest_layout.1 = bf16[64,8,8,128]{3,2,1,0:T(8,128)(2,1)} custom-call(bf16[8,7,64,128]{3,2,1,0:T(8,128)(2,1)S(1)} %bitcast.11, bf16[8,6,64,128]{3,2,1,0:T(8,128)(2,1)S(1)} %bitcast.13, bf16[8,7,64,128]{3,2,1,0:T(8,128)(2,1)S(1)} %bitcast.12, f32[8,8,8,128]{3,2,1,0:T(8,128)S(1)} %get-tuple-element.44.edge_ref), custom_call_target="tpu_custom_call" | custom-call | flops 100000000 | bytes 3000000 | tf_op jit(solution)/shard_map/finest_layout/pallas_call | solution.py:510
  45.9 5.5 %all-to-all-done.in_ref = bf16[64,4,128]{2,1,0:T(4,128)(2,1)S(1)} async-done(((bf16[64,4,128]{2,1,0:T(4,128)(2,1)}), bf16[64,4,128]{2,1,0:T(4,128)(2,1)S(1)}, u32[]{:S(2)}, u32[]{:S(2)}) %all-to-all-start) | async-done | bytes 65568 | tf_op jit(solution)/shard_map/all_to_all | solution.py:509
  51.3 0.9 %coarse_layout.1 = bf16[4,2,32,128]{3,2,1,0:T(8,128)(2,1)} custom-call(bf16[64,4,128]{2,1,0:T(4,128)(2,1)S(1)} %all-to-all-done.in_ref), custom_call_target="tpu_custom_call" | custom-call | flops 1000000 | bytes 200000 | tf_op jit(solution)/shard_map/coarse_layout/pallas_call | solution.py:28
  (2 shorter events, 0.0 us)
Async XLA Ops:
  0.6 12.6 %collective-permute-start = (f32[24,8,128]{2,1,0:T(8,128)}, f32[24,8,128]{2,1,0:T(8,128)S(1)}, u32[]{:S(2)}, u32[]{:S(2)}) collective-permute-start(f32[24,8,128]{2,1,0:T(8,128)} %bitcast.21), channel_id=1, source_target_pairs={{0,4},{4,8},{8,12},{12,16},{16,20},{20,24},{24,28},{28,32},{32,36}... | collective-permute-start | bytes 294920 | tf_op jit(solution)/shard_map/ppermute | solution.py:398
  3.2 2.4 %copy-start.3 = (f32[3,8,8,128]{3,2,1,0:T(8,128)S(1)}, f32[3,8,8,128]{3,2,1,0:T(8,128)}, u32[]{:S(2)}) copy-start(f32[3,8,8,128]{3,2,1,0:T(8,128)} %param.7) | copy-start | bytes 294916
  5.6 10.9 %collective-permute-start.1 = (f32[24,8,128]{2,1,0:T(8,128)S(1)}, f32[24,8,128]{2,1,0:T(8,128)S(1)}, u32[]{:S(2)}, u32[]{:S(2)}) collective-permute-start(f32[24,8,128]{2,1,0:T(8,128)S(1)} %bitcast.23), channel_id=1, source_target_pairs={{0,252},{4,0},{8,4},{12,8},{16,12},{20,16},{24,20},{28,24},{32,28}... | collective-permute-start | bytes 294920 | tf_op jit(solution)/shard_map/ppermute | solution.py:398
  16.7 6.2 %copy-start.2 = (bf16[2,2,2,64,128]{4,3,2,1,0:T(8,128)(2,1)S(1)}, bf16[2,2,2,64,128]{4,3,2,1,0:T(8,128)(2,1)}, u32[]{:S(2)}) copy-start(bf16[2,2,2,64,128]{4,3,2,1,0:T(8,128)(2,1)} %param.10) | copy-start | bytes 393220
  16.7 6.2 %collective-permute-start.2 = (bf16[24,8,128]{2,1,0:T(8,128)(2,1)S(1)}, bf16[24,8,128]{2,1,0:T(8,128)(2,1)S(1)}, u32[]{:S(2)}, u32[]{:S(2)}) collective-permute-start(bf16[24,8,128]{2,1,0:T(8,128)(2,1)S(1)} %get-tuple-element.38.left_ref), channel_id=1, source_target_pairs={{0,3},{1,0},{2,1},{3,2},{4,7},{5,4},{6,5},{7,6},{8,11},{9,8},{10,9... | collective-permute-start | bytes 147464 | tf_op jit(solution)/shard_map/ppermute | solution.py:398
  20.4 6.5 %collective-permute-start.3 = (bf16[24,8,128]{2,1,0:T(8,128)(2,1)S(1)}, bf16[24,8,128]{2,1,0:T(8,128)(2,1)S(1)}, u32[]{:S(2)}, u32[]{:S(2)}) collective-permute-start(bf16[24,8,128]{2,1,0:T(8,128)(2,1)S(1)} %get-tuple-element.41.right_ref), channel_id=1, source_target_pairs={{0,1},{1,2},{2,3},{3,0},{4,5},{5,6},{6,7},{7,4},{8,9},{9,10},{10,1... | collective-permute-start | bytes 147464 | tf_op jit(solution)/shard_map/ppermute | solution.py:398
  23.0 3.9 %copy-start = (bf16[3,3,3,256,256]{4,3,2,1,0:T(8,128)(2,1)S(1)}, bf16[3,3,3,256,256]{4,3,2,1,0:T(8,128)(2,1)}, u32[]{:S(2)}) copy-start(bf16[3,3,3,256,256]{4,3,2,1,0:T(8,128)(2,1)} %param.13) | copy-start | bytes 10616836
  23.0 3.9 %copy-start.1 = (bf16[2,2,2,128,256]{4,3,2,1,0:T(8,128)(2,1)S(1)}, bf16[2,2,2,128,256]{4,3,2,1,0:T(8,128)(2,1)}, u32[]{:S(2)}) copy-start(bf16[2,2,2,128,256]{4,3,2,1,0:T(8,128)(2,1)} %param.12) | copy-start | bytes 1572868
  35.1 16.2 %all-to-all-start = ((bf16[64,4,128]{2,1,0:T(4,128)(2,1)}), bf16[64,4,128]{2,1,0:T(4,128)(2,1)S(1)}, u32[]{:S(2)}, u32[]{:S(2)}) async-start(bf16[64,4,128]{2,1,0:T(4,128)(2,1)} %get-tuple-element.46), calls=%async_computation | async-start | bytes 131072 | tf_op jit(solution)/shard_map/all_to_all | solution.py:509
